TPU v7x, 32 devices: a whole 2x2x4 slice. The times are simulated.
32 devices in a mesh: blk: 4 (over y, x), batch: 8 (over z, core).
Axes of the slice: x: 2, y: 2, z: 4, core: 2. Of those that a mesh axis runs over, the one named last changes fastest.
Arguments:
- hidden_in: bfloat16 [48, 1024, 576], P('batch', 'blk'), may hold values from -6 to 6
- lengths: int32 [48], P('batch'), may hold values from 256 to 1024, as said below
- attn_gain: bfloat16 [576], replicated, may hold values from 0.099609375 to 1.8984375
- w_query: bfloat16 [576, 576], replicated, may hold values from -0.25 to 0.25
- w_key: bfloat16 [576, 192], replicated, may hold values from -0.25 to 0.25
- w_value: bfloat16 [576, 192], replicated, may hold values from -0.25 to 0.25
- w_output: bfloat16 [576, 576], replicated, may hold values from -3 to 3
- mlp_gain: bfloat16 [576], replicated, may hold values from 0.099609375 to 1.8984375
- w_gate: bfloat16 [576, 1536], replicated, may hold values from -0.25 to 0.25
- w_up: bfloat16 [576, 1536], replicated, may hold values from -0.25 to 0.25
- w_down: bfloat16 [1536, 576], replicated, may hold values from -0.15625 to 0.15625
- cotangent: bfloat16 [48, 1024, 576], P('batch', 'blk'), may hold values from -6 to 6
Outputs:
- layer_out: bfloat16 [48, 1024, 576], P('batch', 'blk')
- grad_in: bfloat16 [48, 1024, 576], P('batch', 'blk')
- grad_attn_gain: float32 [576], replicated
- grad_w_query: float32 [576, 576], replicated
- grad_w_key: float32 [576, 192], replicated
- grad_w_value: float32 [576, 192], replicated
- grad_w_output: float32 [576, 576], replicated
- grad_mlp_gain: float32 [576], replicated
- grad_w_gate: float32 [576, 1536], replicated
- grad_w_up: float32 [576, 1536], replicated
- grad_w_down: float32 [1536, 576], replicated
Inputs may be any that keep to these rules, and one draw needn't show every extreme that they name: `lengths`: each sequence holds its tokens in slots 0 to length - 1; in each group of 6 sequences that share an index of batch, one fills all 1024 slots.
All inputs are finite; a program needn't handle non-finite values.
Results may differ from a plain program's by a relative error of at most 0.018.
Values may be sent and summed in bfloat16 or wider, within the bound.
No kernel may reach another device: no remote copies, remote signals or barrier semaphores. Data moves between devices by JAX's collectives and lax.ppermute only.
A program may use at most 256 MiB of HBM per device.

v0:
```python
import math

import jax
import jax.numpy as jnp
from jax import lax
from jax.sharding import PartitionSpec as P

HEADS = 9
KV_HEADS = 3
HEAD_DIM = 64


EPS = 1e-05
THETA = 10000.0
NEGATIVE = -1e30


def rope_table(offset, count):
    half_dim = HEAD_DIM // 2
    frequency = THETA ** (-jnp.arange(half_dim, dtype=jnp.float32) * 2.0 / HEAD_DIM)
    places = (offset + jnp.arange(count, dtype=jnp.int32)).astype(jnp.float32)
    angles = places[:, None] * frequency[None, :]
    return (jnp.cos(angles), jnp.sin(angles))


def rotate(values, cos_table, sin_table):
    half_dim = values.shape[-1] // 2
    leading = values[..., :half_dim]
    trailing = values[..., half_dim:]
    cos_wide = cos_table[:, None, :]
    sin_wide = sin_table[:, None, :]
    return jnp.concatenate(
        [leading * cos_wide - trailing * sin_wide, trailing * cos_wide + leading * sin_wide], -1
    )


def norm_parts(inputs, gain):
    scaled = lax.rsqrt(jnp.mean(inputs * inputs, -1, keepdims=True) + EPS)
    normal = inputs * scaled
    return (normal * gain, normal, scaled)


def norm_back(upstream, gain, normal, scaled):
    inner = upstream * gain
    grad_gain = jnp.sum(upstream * normal, 0)
    grad_inputs = scaled * (inner - normal * jnp.mean(inner * normal, -1, keepdims=True))
    return (grad_inputs, grad_gain)


def block_scores(query_seq, kv_block, block_start, query_places, length, score_scale):
    block_len = kv_block.shape[0]
    kv_width = kv_block.shape[1] // 2
    key_part = kv_block[:, :kv_width].reshape(block_len, KV_HEADS, HEAD_DIM)
    value_part = kv_block[:, kv_width:].reshape(block_len, KV_HEADS, HEAD_DIM)
    scores = (
        jnp.einsum("qkgd,pkd->kgqp", query_seq, key_part, preferred_element_type=jnp.float32)
        * score_scale
    )
    key_places = block_start + jnp.arange(block_len, dtype=jnp.int32)
    allowed = (key_places[None, :] <= query_places[:, None]) & (key_places[None, :] < length)
    return (jnp.where(allowed, scores, NEGATIVE), allowed, key_part, value_part)


def on_device(
    hidden_in,
    lengths,
    attn_gain,
    w_query,
    w_key,
    w_value,
    w_output,
    mlp_gain,
    w_gate,
    w_up,
    w_down,
    cotangent,
):
    seq_count, positions, width = hidden_in.shape
    offset = lax.axis_index("blk") * positions
    row_count = seq_count * positions
    groups = HEADS // KV_HEADS
    kv_width = KV_HEADS * HEAD_DIM
    score_scale = HEAD_DIM ** (-0.5)
    query_places = offset + jnp.arange(positions, dtype=jnp.int32)
    last_query = offset + positions - 1
    valid = (query_places[None, :] < lengths[:, None]).astype(jnp.float32).reshape(row_count, 1)
    inputs = hidden_in.astype(jnp.float32).reshape(row_count, width)
    gain_first = attn_gain.astype(jnp.float32)
    gain_second = mlp_gain.astype(jnp.float32)
    normed_full, normal_first, scaled_first = norm_parts(inputs, gain_first)
    normed = normed_full.astype(jnp.bfloat16)
    cos_table, sin_table = rope_table(offset, positions)
    query_lin = jnp.dot(normed, w_query, preferred_element_type=jnp.float32).reshape(
        seq_count, positions, HEADS, HEAD_DIM
    )
    key_lin = jnp.dot(normed, w_key, preferred_element_type=jnp.float32).reshape(
        seq_count, positions, KV_HEADS, HEAD_DIM
    )
    value_lin = (
        jnp.dot(normed, w_value, preferred_element_type=jnp.float32)
        .astype(jnp.bfloat16)
        .reshape(seq_count, positions, kv_width)
    )
    queries = (
        rotate(query_lin, cos_table, sin_table)
        .astype(jnp.bfloat16)
        .reshape(seq_count, positions, KV_HEADS, groups, HEAD_DIM)
    )
    keys_rot = (
        rotate(key_lin, cos_table, sin_table)
        .astype(jnp.bfloat16)
        .reshape(seq_count, positions, kv_width)
    )
    packed = jnp.concatenate([keys_rot, value_lin], -1)
    initial = (
        jnp.zeros((seq_count, KV_HEADS, groups, positions, HEAD_DIM), jnp.float32),
        jnp.full((seq_count, KV_HEADS, groups, positions), NEGATIVE, jnp.float32),
        jnp.zeros((seq_count, KV_HEADS, groups, positions), jnp.float32),
    )
    kv_piece = lax.all_gather(packed, "blk", axis=1, tiled=True)
    piece_len = kv_piece.shape[1]
    block_len = math.gcd(piece_len, 512)

    def attend_one_sequence(members):
        query_seq, kv_seq, length, summed, running, totals = members

        def attend_visit_block(step_index, current):
            block_start = step_index * block_len

            def attend_compute(current):
                summed, running, totals = current
                kv_block = lax.dynamic_slice_in_dim(kv_seq, step_index * block_len, block_len, 0)
                scores, allowed, key_part, value_part = block_scores(
                    query_seq, kv_block, block_start, query_places, length, score_scale
                )
                new_peak = jnp.maximum(running, jnp.max(scores, -1))
                weights = jnp.where(allowed, jnp.exp(scores - new_peak[..., None]), 0.0)
                fading = jnp.exp(running - new_peak)
                totals = totals * fading + jnp.sum(weights, -1)
                summed = summed * fading[..., None] + jnp.einsum(
                    "kgqp,pkd->kgqd",
                    weights.astype(jnp.bfloat16),
                    value_part,
                    preferred_element_type=jnp.float32,
                )
                return (summed, new_peak, totals)

            active = (block_start <= last_query) & (block_start < length)
            return lax.cond(active, attend_compute, lambda unchanged: unchanged, current)

        return lax.fori_loop(
            0, piece_len // block_len, attend_visit_block, (summed, running, totals)
        )

    attn_sum, attn_peak, attn_total = lax.map(
        attend_one_sequence, (queries, kv_piece, lengths, initial[0], initial[1], initial[2])
    )
    attn_out = attn_sum / attn_total[..., None]
    log_total = attn_peak + jnp.log(attn_total)
    attn_mix = (
        jnp.transpose(attn_out, (0, 3, 1, 2, 4))
        .reshape(row_count, HEADS * HEAD_DIM)
        .astype(jnp.bfloat16)
    )
    middle = inputs + jnp.dot(attn_mix, w_output, preferred_element_type=jnp.float32)
    normed_mid, normal_second, scaled_second = norm_parts(middle, gain_second)
    normed2 = normed_mid.astype(jnp.bfloat16)
    gate = jnp.dot(normed2, w_gate, preferred_element_type=jnp.float32)
    up_part = jnp.dot(normed2, w_up, preferred_element_type=jnp.float32)
    sigmoid_gate = jax.nn.sigmoid(gate)
    activated = gate * sigmoid_gate
    hidden = (activated * up_part).astype(jnp.bfloat16)
    branch = jnp.dot(hidden, w_down, preferred_element_type=jnp.float32)
    layer_out = (
        (valid * (middle + branch)).astype(jnp.bfloat16).reshape(seq_count, positions, width)
    )
    grad_y = cotangent.astype(jnp.float32).reshape(row_count, width) * valid
    grad_branch = grad_y.astype(jnp.bfloat16)
    grad_w_down = jnp.einsum("rf,rd->fd", hidden, grad_branch, preferred_element_type=jnp.float32)
    grad_hidden = jnp.einsum("rd,fd->rf", grad_branch, w_down, preferred_element_type=jnp.float32)
    slope = sigmoid_gate * (1.0 + gate * (1.0 - sigmoid_gate))
    grad_gate = (grad_hidden * up_part * slope).astype(jnp.bfloat16)
    grad_up = (grad_hidden * activated).astype(jnp.bfloat16)
    grad_w_gate = jnp.einsum("rd,rf->df", normed2, grad_gate, preferred_element_type=jnp.float32)
    grad_w_up = jnp.einsum("rd,rf->df", normed2, grad_up, preferred_element_type=jnp.float32)
    grad_normed2 = jnp.einsum(
        "rf,df->rd", grad_gate, w_gate, preferred_element_type=jnp.float32
    ) + jnp.einsum("rf,df->rd", grad_up, w_up, preferred_element_type=jnp.float32)
    grad_mid_norm, grad_mlp_gain = norm_back(
        grad_normed2, gain_second, normal_second, scaled_second
    )
    grad_middle = grad_y + grad_mid_norm
    grad_mix_out = grad_middle.astype(jnp.bfloat16)
    grad_w_output = jnp.einsum(
        "rh,rd->hd", attn_mix, grad_mix_out, preferred_element_type=jnp.float32
    )
    grad_attn = jnp.einsum(
        "rd,hd->rh", grad_mix_out, w_output, preferred_element_type=jnp.float32
    ).astype(jnp.bfloat16)
    grad_heads = jnp.transpose(
        grad_attn.reshape(seq_count, positions, KV_HEADS, groups, HEAD_DIM), (0, 2, 3, 1, 4)
    )
    deltas = jnp.sum(grad_heads.astype(jnp.float32) * attn_out, -1)
    kv_back = lax.all_gather(packed, "blk", axis=1, tiled=True)
    query_zero = jnp.zeros((seq_count, positions, KV_HEADS, groups, HEAD_DIM), jnp.float32)
    back_piece_len = kv_back.shape[1]
    back_block_len = math.gcd(back_piece_len, 512)

    def back_one_sequence(members):
        query_seq, kv_seq, grad_seq, log_seq, delta_seq, length, grad_query_seq = members

        def back_visit_block(step_index, current):
            local_start = step_index * back_block_len
            block_start = 0 + local_start

            def back_compute(current):
                grad_query_acc, grad_kv_acc = current
                kv_block = lax.dynamic_slice_in_dim(kv_seq, local_start, back_block_len, 0)
                scores, allowed, key_part, value_part = block_scores(
                    query_seq, kv_block, block_start, query_places, length, score_scale
                )
                probs = jnp.where(allowed, jnp.exp(scores - log_seq[..., None]), 0.0)
                grad_probs = jnp.einsum(
                    "kgqd,pkd->kgqp", grad_seq, value_part, preferred_element_type=jnp.float32
                )
                grad_scores = (probs * (grad_probs - delta_seq[..., None])).astype(jnp.bfloat16)
                grad_query_acc = (
                    grad_query_acc
                    + jnp.einsum(
                        "kgqp,pkd->qkgd", grad_scores, key_part, preferred_element_type=jnp.float32
                    )
                    * score_scale
                )
                grad_keys = (
                    jnp.einsum(
                        "kgqp,qkgd->pkd", grad_scores, query_seq, preferred_element_type=jnp.float32
                    )
                    * score_scale
                )
                grad_values = jnp.einsum(
                    "kgqp,kgqd->pkd",
                    probs.astype(jnp.bfloat16),
                    grad_seq,
                    preferred_element_type=jnp.float32,
                )
                grad_block = jnp.concatenate(
                    [
                        grad_keys.reshape(back_block_len, kv_width),
                        grad_values.reshape(back_block_len, kv_width),
                    ],
                    -1,
                )
                grad_kv_acc = lax.dynamic_update_slice_in_dim(
                    grad_kv_acc, grad_block, local_start, 0
                )
                return (grad_query_acc, grad_kv_acc)

            active = (block_start <= last_query) & (block_start < length)
            return lax.cond(active, back_compute, lambda unchanged: unchanged, current)

        starting = (grad_query_seq, jnp.zeros((back_piece_len, 2 * kv_width), jnp.float32))
        return lax.fori_loop(0, back_piece_len // back_block_len, back_visit_block, starting)

    grad_query_rot, grad_kv = lax.map(
        back_one_sequence, (queries, kv_back, grad_heads, log_total, deltas, lengths, query_zero)
    )
    grad_kv_own = lax.psum_scatter(
        grad_kv.astype(jnp.bfloat16), "blk", scatter_dimension=1, tiled=True
    ).astype(jnp.float32)
    grad_key_rot = grad_kv_own[..., :kv_width].reshape(seq_count, positions, KV_HEADS, HEAD_DIM)
    grad_value_lin = grad_kv_own[..., kv_width:].reshape(row_count, kv_width).astype(jnp.bfloat16)
    grad_key_lin = (
        rotate(grad_key_rot, cos_table, -sin_table)
        .reshape(row_count, kv_width)
        .astype(jnp.bfloat16)
    )
    grad_query_lin = (
        rotate(grad_query_rot.reshape(seq_count, positions, HEADS, HEAD_DIM), cos_table, -sin_table)
        .reshape(row_count, HEADS * HEAD_DIM)
        .astype(jnp.bfloat16)
    )
    grad_w_query = jnp.einsum(
        "rd,rh->dh", normed, grad_query_lin, preferred_element_type=jnp.float32
    )
    grad_w_key = jnp.einsum("rd,rh->dh", normed, grad_key_lin, preferred_element_type=jnp.float32)
    grad_w_value = jnp.einsum(
        "rd,rh->dh", normed, grad_value_lin, preferred_element_type=jnp.float32
    )
    grad_normed = jnp.einsum(
        "rh,dh->rd", grad_query_lin, w_query, preferred_element_type=jnp.float32
    )
    grad_normed = grad_normed + jnp.einsum(
        "rh,dh->rd", grad_key_lin, w_key, preferred_element_type=jnp.float32
    )
    grad_normed = grad_normed + jnp.einsum(
        "rh,dh->rd", grad_value_lin, w_value, preferred_element_type=jnp.float32
    )
    grad_in_norm, grad_attn_gain = norm_back(grad_normed, gain_first, normal_first, scaled_first)
    grad_in = (grad_middle + grad_in_norm).astype(jnp.bfloat16).reshape(seq_count, positions, width)
    summed = lax.psum(
        (
            grad_attn_gain,
            grad_w_query,
            grad_w_key,
            grad_w_value,
            grad_w_output,
            grad_mlp_gain,
            grad_w_gate,
            grad_w_up,
            grad_w_down,
        ),
        ("blk", "batch"),
    )
    return (
        layer_out,
        grad_in,
        summed[0],
        summed[1],
        summed[2],
        summed[3],
        summed[4],
        summed[5],
        summed[6],
        summed[7],
        summed[8],
    )


def solution(mesh):
    return jax.shard_map(
        on_device,
        mesh=mesh,
        in_specs=(
            P("batch", "blk", None),
            P("batch"),
            P(),
            P(),
            P(),
            P(),
            P(),
            P(),
            P(),
            P(),
            P(),
            P("batch", "blk", None),
        ),
        out_specs=(
            P("batch", "blk", None),
            P("batch", "blk", None),
            P(),
            P(),
            P(),
            P(),
            P(),
            P(),
            P(),
            P(),
            P(),
        ),
        check_vma=False,
    )
```

profile of v0, /device:TPU:0, one launch (start us, length us, event | category | flops | bytes accessed | tf_op | source)
XLA Modules:
  0.0 830.3 jit_solution(12718051228498015469)
XLA Ops:
  7.2 4.3 copy.62
  12.4 5.3 copy.69
  39.1 5.5 copy.72
  50.0 54.4 %all-gather.2.cloned.1.call-done = bf16[6,1024,384]{1,0,2:T(8,128)(2,1)} async-done(((bf16[6,256,384]{1,0,2:T(8,128)(2,1)}), bf16[6,1024,384]{1,0,2:T(8,128)(2,1)}) %all-gather.2.cloned.1.call-update) | async-done | bytes 4718608 | tf_op jit(solution)/shard_map/all_gather | solution.py:120
  104.4 7.5 copy.66
  111.9 144.6 %while.63 = (s32[]{:T(128)}, f32[6,3,3,256,64]{3,0,4,2,1:T(8,128)}, f32[6,3,3,256]{3,2,1,0:T(4,128)}, f32[6,3,3,256]{3,2,1,0:T(4,128)S(1)}, s32[6]{0:T(128)S(1)}...) while((s32[]{:T(128)}, f32[6,3,3,256,64]{3,0,4,2,1:T(8,128)}, ...), condition=%wide.region_8.9_spmd.clone, body=%wide.region_1.8_spmd.clone.sunk | while | flops 317888768 | bytes 22668936 | solution.py:155
  114.8 5.8 while.66
  115.4 4.5 conditional.5
  121.2 14.2 %dynamic_update_slice.37 = f32[6,3,3,256,64]{3,0,4,2,1:T(8,128)} dynamic-update-slice(f32[6,3,3,256,64]{3,0,4,2,1:T(8,128)} %get-tuple-element.1207, f32[1,3,3,256,64]{3,0,4,2,1:T(1,128)S(1)} %copy.111, s32[]{:T(128)S(6)} %copy.154, s32[]{:T(128)} %constant.132.clone.1..sunk, s32[]{:T(128)} %constant.132.clone.1..sunk, s32[]{:T(128)} %constant.132.clone.1..sunk, s32[]{:T(128)} %constant.132.clone.1..sunk) | dynamic-update-slice | bytes 1179652 | tf_op jit(solution)/shard_map/while/body/jit(dynamic_update_index_in_dim)/dynamic_update_slice | solution.py:155
  138.9 5.8 while.66
  139.5 4.5 conditional.5
  145.3 14.2 %dynamic_update_slice.37 = f32[6,3,3,256,64]{3,0,4,2,1:T(8,128)} dynamic-update-slice(f32[6,3,3,256,64]{3,0,4,2,1:T(8,128)} %get-tuple-element.1207, f32[1,3,3,256,64]{3,0,4,2,1:T(1,128)S(1)} %copy.111, s32[]{:T(128)S(6)} %copy.154, s32[]{:T(128)} %constant.132.clone.1..sunk, s32[]{:T(128)} %constant.132.clone.1..sunk, s32[]{:T(128)} %constant.132.clone.1..sunk, s32[]{:T(128)} %constant.132.clone.1..sunk) | dynamic-update-slice | bytes 1179652 | tf_op jit(solution)/shard_map/while/body/jit(dynamic_update_index_in_dim)/dynamic_update_slice | solution.py:155
  162.9 5.8 while.66
  163.6 4.5 conditional.5
  169.4 14.2 %dynamic_update_slice.37 = f32[6,3,3,256,64]{3,0,4,2,1:T(8,128)} dynamic-update-slice(f32[6,3,3,256,64]{3,0,4,2,1:T(8,128)} %get-tuple-element.1207, f32[1,3,3,256,64]{3,0,4,2,1:T(1,128)S(1)} %copy.111, s32[]{:T(128)S(6)} %copy.154, s32[]{:T(128)} %constant.132.clone.1..sunk, s32[]{:T(128)} %constant.132.clone.1..sunk, s32[]{:T(128)} %constant.132.clone.1..sunk, s32[]{:T(128)} %constant.132.clone.1..sunk) | dynamic-update-slice | bytes 1179652 | tf_op jit(solution)/shard_map/while/body/jit(dynamic_update_index_in_dim)/dynamic_update_slice | solution.py:155
  187.0 5.8 while.66
  187.7 4.5 conditional.5
  193.5 14.2 %dynamic_update_slice.37 = f32[6,3,3,256,64]{3,0,4,2,1:T(8,128)} dynamic-update-slice(f32[6,3,3,256,64]{3,0,4,2,1:T(8,128)} %get-tuple-element.1207, f32[1,3,3,256,64]{3,0,4,2,1:T(1,128)S(1)} %copy.111, s32[]{:T(128)S(6)} %copy.154, s32[]{:T(128)} %constant.132.clone.1..sunk, s32[]{:T(128)} %constant.132.clone.1..sunk, s32[]{:T(128)} %constant.132.clone.1..sunk, s32[]{:T(128)} %constant.132.clone.1..sunk) | dynamic-update-slice | bytes 1179652 | tf_op jit(solution)/shard_map/while/body/jit(dynamic_update_index_in_dim)/dynamic_update_slice | solution.py:155
  211.1 5.8 while.66
  211.8 4.5 conditional.5
  217.6 14.2 %dynamic_update_slice.37 = f32[6,3,3,256,64]{3,0,4,2,1:T(8,128)} dynamic-update-slice(f32[6,3,3,256,64]{3,0,4,2,1:T(8,128)} %get-tuple-element.1207, f32[1,3,3,256,64]{3,0,4,2,1:T(1,128)S(1)} %copy.111, s32[]{:T(128)S(6)} %copy.154, s32[]{:T(128)} %constant.132.clone.1..sunk, s32[]{:T(128)} %constant.132.clone.1..sunk, s32[]{:T(128)} %constant.132.clone.1..sunk, s32[]{:T(128)} %constant.132.clone.1..sunk) | dynamic-update-slice | bytes 1179652 | tf_op jit(solution)/shard_map/while/body/jit(dynamic_update_index_in_dim)/dynamic_update_slice | solution.py:155
  235.2 5.8 while.66
  235.9 4.5 conditional.5
  241.6 14.2 %dynamic_update_slice.37 = f32[6,3,3,256,64]{3,0,4,2,1:T(8,128)} dynamic-update-slice(f32[6,3,3,256,64]{3,0,4,2,1:T(8,128)} %get-tuple-element.1207, f32[1,3,3,256,64]{3,0,4,2,1:T(1,128)S(1)} %copy.111, s32[]{:T(128)S(6)} %copy.154, s32[]{:T(128)} %constant.132.clone.1..sunk, s32[]{:T(128)} %constant.132.clone.1..sunk, s32[]{:T(128)} %constant.132.clone.1..sunk, s32[]{:T(128)} %constant.132.clone.1..sunk) | dynamic-update-slice | bytes 1179652 | tf_op jit(solution)/shard_map/while/body/jit(dynamic_update_index_in_dim)/dynamic_update_slice | solution.py:155
  266.6 6.5 fusion.48
  273.1 6.6 fusion.49
  279.7 16.6 %multiply_convert_fusion = (bf16[1536,1536]{1,0:T(8,128)(2,1)}, bf16[1536,1536]{1,0:T(8,128)(2,1)}, bf16[1536,1536]{1,0:T(8,128)(2,1)}) fusion(f32[1536,1536]{1,0:T(8,128)} %fusion.48, f32[1536,1536]{1,0:T(8,128)} %fusion.49, bf16[1536,576]{0,1:T(8,128)(2,1)S(1)} %copy-done, f32[1536,576]{0,1:T(8,128)S(1)} %copy-done.11, f32[1536]{0:T(1024)S(1)} %copy-done.50), kind=kOutput, calls=%fused_computation.55 | convolution fusion | flops 2755067904 | bytes 38344704 | tf_op jit(solution)/shard_map/rd,fd->rf/dot_general | solution.py:180
  296.3 5.2 fusion.50
  319.5 106.7 %while.65 = (s32[]{:T(128)}, f32[6,256,3,3,64]{1,4,3,2,0:T(8,128)}, bf16[6,1024,384]{1,2,0:T(8,128)(2,1)}, s32[6]{0:T(128)S(1)}, bf16[6,1024,384]{1,2,0:T(8,128)...) while((s32[]{:T(128)}, f32[6,256,3,3,64]{1,4,3,2,0:T(8,128)}, ...), condition=%wide.region_17.18_spmd.clone, body=%wide.region_12.17_spmd.clone.sunk | while | flops 770672384 | bytes 40985336 | solution.py:264
  325.8 8.5 %while.67 = (s32[]{:T(128)}, f32[256,3,3,64]{0,3,2,1:T(8,128)S(1)}, bf16[1024,384]{0,1:T(8,128)(2,1)}, s32[]{:T(128)}, s32[]{:T(128)}, /*index=5*/bf16[1024,384]...) while((s32[]{:T(128)}, f32[256,3,3,64]{0,3,2,1:T(8,128)S(1)}, ...), condition=%wide.region_16.16_spmd, body=%wide.region_13.15_spmd.sunk | while | flops 770672128 | bytes 34047416 | solution.py:262
  326.5 7.1 conditional.4
  343.6 8.5 %while.67 = (s32[]{:T(128)}, f32[256,3,3,64]{0,3,2,1:T(8,128)S(1)}, bf16[1024,384]{0,1:T(8,128)(2,1)}, s32[]{:T(128)}, s32[]{:T(128)}, /*index=5*/bf16[1024,384]...) while((s32[]{:T(128)}, f32[256,3,3,64]{0,3,2,1:T(8,128)S(1)}, ...), condition=%wide.region_16.16_spmd, body=%wide.region_13.15_spmd.sunk | while | flops 770672128 | bytes 34047416 | solution.py:262
  344.3 7.1 conditional.4
  361.4 8.5 %while.67 = (s32[]{:T(128)}, f32[256,3,3,64]{0,3,2,1:T(8,128)S(1)}, bf16[1024,384]{0,1:T(8,128)(2,1)}, s32[]{:T(128)}, s32[]{:T(128)}, /*index=5*/bf16[1024,384]...) while((s32[]{:T(128)}, f32[256,3,3,64]{0,3,2,1:T(8,128)S(1)}, ...), condition=%wide.region_16.16_spmd, body=%wide.region_13.15_spmd.sunk | while | flops 770672128 | bytes 34047416 | solution.py:262
  362.1 7.1 conditional.4
  379.2 8.5 %while.67 = (s32[]{:T(128)}, f32[256,3,3,64]{0,3,2,1:T(8,128)S(1)}, bf16[1024,384]{0,1:T(8,128)(2,1)}, s32[]{:T(128)}, s32[]{:T(128)}, /*index=5*/bf16[1024,384]...) while((s32[]{:T(128)}, f32[256,3,3,64]{0,3,2,1:T(8,128)S(1)}, ...), condition=%wide.region_16.16_spmd, body=%wide.region_13.15_spmd.sunk | while | flops 770672128 | bytes 34047416 | solution.py:262
  379.9 7.1 conditional.4
  397.0 8.5 %while.67 = (s32[]{:T(128)}, f32[256,3,3,64]{0,3,2,1:T(8,128)S(1)}, bf16[1024,384]{0,1:T(8,128)(2,1)}, s32[]{:T(128)}, s32[]{:T(128)}, /*index=5*/bf16[1024,384]...) while((s32[]{:T(128)}, f32[256,3,3,64]{0,3,2,1:T(8,128)S(1)}, ...), condition=%wide.region_16.16_spmd, body=%wide.region_13.15_spmd.sunk | while | flops 770672128 | bytes 34047416 | solution.py:262
  397.7 7.1 conditional.4
  414.7 8.5 %while.67 = (s32[]{:T(128)}, f32[256,3,3,64]{0,3,2,1:T(8,128)S(1)}, bf16[1024,384]{0,1:T(8,128)(2,1)}, s32[]{:T(128)}, s32[]{:T(128)}, /*index=5*/bf16[1024,384]...) while((s32[]{:T(128)}, f32[256,3,3,64]{0,3,2,1:T(8,128)S(1)}, ...), condition=%wide.region_16.16_spmd, body=%wide.region_13.15_spmd.sunk | while | flops 770672128 | bytes 34047416 | solution.py:262
  415.4 7.1 conditional.4
  441.7 4.8 fusion.53
  446.5 4.8 fusion.54
  451.3 4.7 fusion.41
  456.0 84.5 %reduce-scatter.2.cloned.1.call-done = bf16[6,256,384]{1,2,0:T(8,128)(2,1)} async-done(((bf16[6,1024,384]{1,2,0:T(8,128)(2,1)}), bf16[6,256,384]{1,2,0:T(8,128)(2,1)}) %reduce-scatter.2.cloned.1.call-update) | async-done | bytes 1179664 | tf_op jit(solution)/shard_map/reduce_scatter | solution.py:267
  546.4 6.2 multiply_convert_fusion.3
  572.9 40.5 %all-reduce = (f32[576]{0:T(1024)}, f32[576]{0:T(1024)}) all-reduce(f32[576]{0:T(1024)S(1)} %get-tuple-element.672, f32[576]{0:T(1024)S(1)} %copy-done.52), channel_id=1, replica_groups=mesh['blk'=4,'batch'=8] {'blk','batch'}, use_global_device_ids=true, to_apply=%region_21.22 | all-reduce | flops 1152 | bytes 9216 | tf_op jit(solution)/shard_map/psum | solution.py:300
  613.5 195.3 %all-reduce.4.cloned.1.call-done = (f32[576,576]{1,0:T(8,128)}, f32[576,192]{0,1:T(8,128)}, f32[576,192]{0,1:T(8,128)}, f32[576,576]{1,0:T(8,128)}, f32[576,1536...) async-done(((f32[576,576]{1,0:T(8,128)}, f32[576,192]{0,1:T(8,128)}, f32[576,192]{0,1:T(8,128)}, f32[576,576]{1,0:T(8,128)}, f32[576,1536]{1,0:T(8,128)}, ...) | async-done | bytes 14155792 | tf_op jit(solution)/shard_map/psum | solution.py:300
  (499 shorter events, 259.5 us)
Async XLA Ops:
  7.2 272.5 %copy-start = (bf16[1536,576]{0,1:T(8,128)(2,1)S(1)}, bf16[1536,576]{0,1:T(8,128)(2,1)}, u32[]{:S(2)}) copy-start(bf16[1536,576]{0,1:T(8,128)(2,1)} %param.34) | copy-start | bytes 5308420
  7.2 4.3 copy-start.8
  7.2 97.2 %all-gather.2.cloned.1.call-start = ((), (), s32[]{:S(2)}) async-start(), calls=%async_computation.1 | async-start | bytes 7864320 | tf_op jit(solution)/shard_map/all_gather | solution.py:120
  12.4 5.3 copy-start.53
  17.7 6.5 copy-start.46
  19.0 5.2 copy-start.44
  21.5 5.1 copy-start.9
  21.5 6.8 copy-start.55
  26.6 3.4 copy-start.26
  29.7 4.7 copy-start.54
  31.5 509.0 %reduce-scatter.2.cloned.1.call-start = ((), (), s32[]{:S(2)}) async-start(), calls=%async_computation.2 | async-start | bytes 5898240 | tf_op jit(solution)/shard_map/reduce_scatter | solution.py:267
  39.1 5.5 copy-start.56
  50.0 62.0 %copy-start.43 = (f32[6,3,3,256]{3,2,1,0:T(4,128)S(1)}, f32[6,3,3,256]{3,2,1,0:T(4,128)}, u32[]{:S(2)}) copy-start(f32[6,3,3,256]{3,2,1,0:T(4,128)} %custom-call.2) | copy-start | bytes 165892
  256.6 2.9 copy-start.39
  256.6 3.4 copy-start.38
  260.0 3.8 copy-start.16
  263.9 42.3 %copy-start.6 = (f32[1536,576]{0,1:T(8,128)}, f32[1536,576]{0,1:T(8,128)S(1)}, u32[]{:S(2)}) copy-start(f32[1536,576]{0,1:T(8,128)S(1)} %get-tuple-element.790) | copy-start | bytes 10616836
  263.9 2.8 copy-start.57
  266.6 6.5 copy-start.29
  266.6 6.5 copy-start.58
  273.1 6.6 copy-start.11
  273.1 6.6 copy-start.50
  296.3 5.2 copy-start.59
  296.3 5.2 copy-start.60
  301.5 4.0 copy-start.48
  313.9 4.0 copy-start.7
  426.3 382.5 %all-reduce.4.cloned.1.call-start = ((), (), s32[]{:S(2)}) async-start(), calls=%async_computation.3 | async-start | bytes 29097984 | tf_op jit(solution)/shard_map/psum | solution.py:300
  433.1 3.0 copy-start.18
  436.1 2.8 copy-start.14
  436.1 2.8 copy-start.17
  436.1 5.5 slice-start.2
  438.9 7.5 slice-start
  441.7 4.8 slice-start.1
  441.7 9.6 %slice-start.4 = ((s8[4718592]{0:T(1024)(128)(4,1)}), s8[524288]{0:T(1024)(128)(4,1)S(1)}, s32[]{:S(2)}) async-start(s8[4718592]{0:T(1024)(128)(4,1)} %bitcast.253), calls=%async_computation.8 | async-start | bytes 1048576
  446.5 4.8 copy-start.12
  446.5 4.8 copy-start.51
  446.5 4.8 slice-start.5
  540.5 2.8 copy-start.19
  554.9 4.1 copy-start.32
  558.9 2.8 copy-start.28
  559.0 3.0 copy-start.22
  559.0 3.0 copy-start.35
  566.7 6.2 copy-start.52
  808.8 4.6 copy-start.40
  808.8 5.4 copy-start.33
  808.8 6.5 copy-start.25
  815.3 3.3 copy-start.24
  818.5 3.3 copy-start.23
  (37 other events, 66.2 us)
Sparse Core Ops, SparseCore 0:
  31.7 72.7 all-gather.1
  426.4 114.1 reduce-scatter.1
  548.1 260.6 all-reduce.3
where the time goes:
time: 838 us; the launch traced here: 830 us
  waiting for transfers between devices  334 us (40%)
  local copies, waits for them, and re-layouts  253 us (30%)
  matrix products  128 us (15%)
  other arithmetic  40.6 us (5%)
  blocking collectives  40.5 us (5%)
  loops' own time  18.6 us (2%)
  between operations  14.6 us (2%)
    psum x1, waiting for transfers between devices, on_device(): lax.psum((grad_attn_gain, grad_w_query, grad_w_key, grad_w_value, grad_w_...  195 us
    dynamic_update_slice x18, local copies, waits for them, and re-layouts, on_device(): lax.map(attend_one_sequence, (queries, kv_piece, lengths, initial[0], ini...  92.3 us
    reduce_scatter x1, waiting for transfers between devices, on_device(): lax.psum_scatter(grad_kv.astype(jnp.bfloat16), 'blk', scatter_dimension=1...  84.5 us
    all_gather x1, waiting for transfers between devices, on_device(): kv_piece = lax.all_gather(packed, 'blk', axis=1, tiled=True)  54.4 us
    unnamed x144, local copies, waits for them, and re-layouts  46.7 us
    psum x1, blocking collectives, on_device(): lax.psum((grad_attn_gain, grad_w_query, grad_w_key, grad_w_value, grad_w_...  40.5 us
    squeeze x48, local copies, waits for them, and re-layouts, on_device(): lax.map(attend_one_sequence, (queries, kv_piece, lengths, initial[0], ini...  30.7 us
    dynamic_update_slice x12, local copies, waits for them, and re-layouts, on_device(): lax.map(back_one_sequence, (queries, kv_back, grad_heads, log_total, delt...  17.8 us
  transfers between devices with their start and end apart: 3, of which 3 were waited for; matrix products, arithmetic and copies ran while one was open for 8% of the time, Pallas kernels for 0%

commit v1 on v0

v1 whole, which is shorter than its diff:
```python
import functools

import jax
import jax.numpy as jnp
import numpy as np
from jax import lax
from jax.experimental import pallas as pl
from jax.experimental.pallas import tpu as pltpu
from jax.sharding import PartitionSpec as P

HEADS = 9
KV_HEADS = 3
HEAD_DIM = 64
GROUPS = HEADS // KV_HEADS
HALF = HEAD_DIM // 2
KV_WIDTH = KV_HEADS * HEAD_DIM
Q_WIDTH = HEADS * HEAD_DIM

EPS = 1e-05
THETA = 10000.0
NEGATIVE = -1e30
LANES = 128
F32 = jnp.float32
BF16 = jnp.bfloat16
VMEM_LIMIT = 60 * 1024 * 1024

NN = (((1,), (0,)), ((), ()))
NT = (((1,), (1,)), ((), ()))
TN = (((0,), (0,)), ((), ()))


def dot(a, b, dims=NN):
    return lax.dot_general(a, b, dims, preferred_element_type=F32)


def call(
    kernel, name, grid, in_specs, out_specs, out_shape, scratch=(), flops=0, bytes_accessed=0, after=()
):
    count, more = len(in_specs), len(after)

    def body(info, *refs):
        kernel(info, *refs[:count], *refs[count + more :])

    made = pl.pallas_call(
        body,
        grid_spec=pltpu.PrefetchScalarGridSpec(
            num_scalar_prefetch=1,
            grid=grid,
            in_specs=list(in_specs) + [pl.BlockSpec(memory_space=pl.ANY)] * more,
            out_specs=out_specs,
            scratch_shapes=list(scratch),
        ),
        out_shape=out_shape,
        compiler_params=pltpu.CompilerParams(
            dimension_semantics=("arbitrary",), vmem_limit_bytes=VMEM_LIMIT
        ),
        cost_estimate=pl.CostEstimate(
            flops=int(flops), bytes_accessed=int(bytes_accessed), transcendentals=0
        ),
        name=name,
    )
    return lambda *operands: made(*operands, *after)


def per_step(*shape):
    zeros = (0,) * len(shape)
    return pl.BlockSpec((1,) + shape, lambda s, info: (s,) + zeros)


def whole(*shape):
    zeros = (0,) * len(shape)
    return pl.BlockSpec(shape, lambda s, info: zeros, pipeline_mode=pl.Buffered(1))


def kept(*shape):
    zeros = (0,) * len(shape)
    return pl.BlockSpec(shape, lambda s, info: zeros)


def valid_rows(info, slot, block, positions):
    return jnp.clip(info[slot] - block * positions, 0, positions)


def first_bit(count, slots):
    return slots + 1 + count * slots


def pick(count, info, *refs):
    for distance in range(count):
        refs[count + distance][...] = refs[distance][...]


def put(count, last, info, *refs):
    distance = info[last + pl.program_id(0)]
    for which in range(count):

        @pl.when(distance == which)
        def _():
            refs[count][...] = refs[which][...]


def rotate(lin, cos, sin, heads, store):
    for head in range(heads):
        low = head * HEAD_DIM
        lead, trail = lin[low : low + HALF], lin[low + HALF : low + HEAD_DIM]
        store(low, (lead * cos - trail * sin).astype(BF16))
        store(low + HALF, (trail * cos + lead * sin).astype(BF16))


def front(positions, count, info, *refs):
    x_refs, refs = refs[:count], refs[count:]
    gain_ref, wq_ref, wkv_ref, cos_ref, sin_ref = refs[:5]
    normed_ref, q_ref, kv_ref, mix_ref, log_ref, stat, acc = refs[5:]
    slot = pl.program_id(0)
    blk = info[pl.num_programs(0)]
    blocks = lax.div(info[slot] + positions - 1, positions)

    for distance in range(count):
        block = blk ^ distance

        @pl.when(block < blocks)
        def _():
            x = x_refs[distance][0].astype(F32)
            scaled = lax.rsqrt(jnp.mean(x * x, axis=0, keepdims=True) + EPS)
            normed = (x * scaled * gain_ref[...]).astype(BF16)
            normed_ref[0, block] = normed
            cos, sin = cos_ref[block], sin_ref[block]
            lin = dot(wkv_ref[...], normed)

            def store_kv(low, value):
                kv_ref[0, block, low : low + HALF] = value

            rotate(lin, cos, sin, KV_HEADS, store_kv)
            kv_ref[0, block, KV_WIDTH:] = lin[KV_WIDTH:].astype(BF16)

            def store_q(low, value):
                q_ref[0, block, low : low + HALF] = value

            rotate(dot(wq_ref[...], normed) * (HEAD_DIM**-0.5), cos, sin, HEADS, store_q)

    def visit(block, other, diagonal):
        if diagonal:
            mask = causal_mask(positions, GROUPS)
        for group in range(KV_HEADS):
            low = group * HEAD_DIM
            key = kv_ref[0, other, low : low + HEAD_DIM]
            value = kv_ref[0, other, KV_WIDTH + low : KV_WIDTH + low + HEAD_DIM]
            scores = dot(key, heads_side_by_side(q_ref, block, group), TN)
            if diagonal:
                scores = jnp.where(mask, scores, NEGATIVE)
            peak = jnp.max(scores, axis=0, keepdims=True)
            if not diagonal:
                old = stat[group : group + 1]
                peak = jnp.maximum(peak, old)
            weights = jnp.exp(scores - peak)
            total = jnp.sum(weights, axis=0, keepdims=True)
            summed = dot(value, weights.astype(BF16))
            if not diagonal:
                fade = jnp.exp(old - peak)
                total = total + stat[KV_HEADS + group : KV_HEADS + group + 1] * fade
                summed = summed + acc[low : low + HEAD_DIM] * fade
            stat[group : group + 1] = peak
            stat[KV_HEADS + group : KV_HEADS + group + 1] = total
            acc[low : low + HEAD_DIM] = summed

    def one_block(block, carry):
        visit(block, block, True)

        def one_pair(other, carry):
            visit(block, other, False)
            return carry

        lax.fori_loop(0, block, one_pair, 0)
        log_ref[0, block] = stat[:KV_HEADS] + jnp.log(stat[KV_HEADS:])
        for group in range(KV_HEADS):
            low = group * HEAD_DIM
            share = 1.0 / stat[KV_HEADS + group : KV_HEADS + group + 1]
            mix = (acc[low : low + HEAD_DIM] * share).astype(BF16)
            for place in range(GROUPS):
                row = (group * GROUPS + place) * HEAD_DIM
                mix_ref[0, block, row : row + HEAD_DIM] = mix[
                    :, place * positions : (place + 1) * positions
                ]
        return carry

    lax.fori_loop(0, blocks, one_block, 0)


def causal_mask(positions, copies):
    keys = lax.broadcasted_iota(jnp.int32, (positions, positions), 0)
    queries = lax.broadcasted_iota(jnp.int32, (positions, positions), 1)
    return jnp.concatenate([keys <= queries] * copies, 1)


def heads_side_by_side(ref, block, group):
    first = group * GROUPS * HEAD_DIM
    return jnp.concatenate(
        [ref[0, block, first + p * HEAD_DIM : first + (p + 1) * HEAD_DIM] for p in range(GROUPS)],
        1,
    )


def pieces_of(columns):
    return [(start, min(LANES, columns - start)) for start in range(0, columns, LANES)]


class Parts:
    def __init__(self, halves, count, blk):
        self.halves, self.count, self.blk = halves, count, blk
        self.size = halves[0].shape[0] // count

    def write(self, row, value):
        done, rows = 0, value.shape[0]
        while done < rows:
            part, inside = divmod(row + done, self.size)
            take = min(self.size - inside, rows - done)
            half, part = divmod(part, self.count)
            start = pl.multiple_of((part ^ self.blk) * self.size + inside, 16)
            self.halves[half][pl.ds(start, take)] = value[done : done + take]
            done += take


def pack_into(parts, row, acc):
    rows, columns = acc.shape
    for start, width in pieces_of(columns):
        part = acc[:, start : start + width].astype(BF16)
        if width < LANES:
            half = rows // 2
            part = jnp.concatenate([part[:half], part[half:]], 1)
        parts.write(row, part)
        row += part.shape[0]
    return row


def gain_rows(acc):
    ones = jnp.ones((16, acc.shape[1]), BF16)
    sums = dot(ones, acc[...].astype(BF16), NT)[:1]
    parts = [sums[:, start : start + width] for start, width in pieces_of(sums.shape[1])]
    short = LANES - parts[-1].shape[1]
    if short:
        parts[-1] = jnp.concatenate([parts[-1], jnp.zeros((1, short), F32)], 1)
    return parts


def pack_all(info, bit_at, count, blk, mine_ref, send_ref, accs, last=None):
    def fill(halves):
        parts = Parts(halves, count, blk)
        row = 0
        for acc in accs:
            row = pack_into(parts, row, acc)
        if last is not None:
            parts.write(row, last)
            row += last.shape[0]
        rest = 2 * mine_ref.shape[0] - row
        if rest:
            parts.write(row, jnp.zeros((rest, LANES), BF16))

    pl.when(info[bit_at] == 0)(lambda: fill((mine_ref, send_ref)))
    pl.when(info[bit_at] != 0)(lambda: fill((send_ref, mine_ref)))


def packed_rows(rows, columns):
    return rows * columns // LANES


def feed_forward(
    positions,
    chunk,
    count,
    slots,
    info,
    *refs,
):
    x_refs, cot_refs, refs = refs[:count], refs[count : 2 * count], refs[2 * count :]
    ins, out_refs, rest = refs[:10], refs[10 : 10 + count], refs[10 + count :]
    feed_forward_step(
        positions, chunk, count, slots, info, x_refs, cot_refs, out_refs, *ins, *rest
    )


def feed_forward_step(
    positions,
    chunk,
    count,
    slots,
    info,
    x_refs,
    cot_refs,
    out_refs,
    mix_ref,
    gain_ref,
    wo_t_ref,
    wo_ref,
    wg_t_ref,
    wg_ref,
    wu_t_ref,
    wu_ref,
    wd_t_ref,
    wd_ref,
    mid_ref,
    gattn_ref,
    delta_ref,
    mine_ref,
    send_ref,
    gain_sum_ref,
    acc_gate,
    acc_up,
    acc_down,
    acc_out,
    x_now,
    cot_now,
    out_now,
):
    step = pl.program_id(0)
    distance, slot = lax.div(step, slots), lax.rem(step, slots)
    rows = valid_rows(info, slot, info[slots] ^ distance, positions)
    width = x_now.shape[0]
    hidden_width = wg_ref.shape[1]

    @pl.when(step == 0)
    def _():
        acc_gate[...] = jnp.zeros_like(acc_gate)
        acc_up[...] = jnp.zeros_like(acc_up)
        acc_down[...] = jnp.zeros_like(acc_down)
        acc_out[...] = jnp.zeros_like(acc_out)
        gain_sum_ref[...] = jnp.zeros_like(gain_sum_ref)

    @pl.when(rows <= 0)
    def _():
        out_now[...] = jnp.zeros_like(out_now)

    for which in range(count):

        @pl.when(jnp.logical_and(rows > 0, distance == which))
        def _():
            x_now[...] = x_refs[which][0]
            cot_now[...] = cot_refs[which][0]

    @pl.when(rows > 0)
    def _():
        lane = lax.broadcasted_iota(jnp.int32, (1, positions), 1)
        valid = (lane < rows).astype(F32)
        mix = mix_ref[0, 0]
        middle = x_now[...].astype(F32) + dot(wo_t_ref[...], mix)
        scaled = lax.rsqrt(jnp.mean(middle * middle, axis=0, keepdims=True) + EPS)
        normal = middle * scaled
        gain = gain_ref[...]
        normed = (normal * gain).astype(BF16)
        grad_y = cot_now[...].astype(F32) * valid
        grad_low = grad_y.astype(BF16)
        branch = jnp.zeros((width, positions), F32)
        grad_normed = jnp.zeros((width, positions), F32)
        for start in range(0, hidden_width, chunk):
            part = slice(start, start + chunk)
            gate = dot(wg_t_ref[part], normed)
            up = dot(wu_t_ref[part], normed)
            grad_hidden = dot(wd_ref[part], grad_low)
            sig = 1.0 / (1.0 + jnp.exp(-gate))
            act = gate * sig
            hidden = (act * up).astype(BF16)
            grad_gate = (grad_hidden * up * (sig * (1.0 + gate * (1.0 - sig)))).astype(BF16)
            grad_up = (grad_hidden * act).astype(BF16)
            branch = branch + dot(wd_t_ref[:, part], hidden)
            grad_normed = grad_normed + dot(wg_ref[:, part], grad_gate)
            grad_normed = grad_normed + dot(wu_ref[:, part], grad_up)
            acc_down[:, part] += dot(grad_low, hidden, NT)
            acc_gate[:, part] += dot(normed, grad_gate, NT)
            acc_up[:, part] += dot(normed, grad_up, NT)
        out_now[...] = (valid * (middle + branch)).astype(BF16)
        gain_sum_ref[...] += grad_normed * normal
        inner = grad_normed * gain
        mean = jnp.mean(inner * normal, axis=0, keepdims=True)
        grad_middle = grad_y + scaled * (inner - normal * mean)
        mid_ref[0, 0] = grad_middle.astype(BF16)
        grad_mid_low = grad_middle.astype(BF16)
        acc_out[...] += dot(mix, grad_mid_low, NT)
        grad_attn = dot(wo_ref[...], grad_mid_low).astype(BF16)
        gattn_ref[0, 0] = grad_attn
        product = grad_attn.astype(F32) * mix.astype(F32)
        for head in range(HEADS):
            part = slice(head * HEAD_DIM, (head + 1) * HEAD_DIM)
            group, place = head // GROUPS, head % GROUPS
            delta_ref[0, 0, group : group + 1, place * positions : (place + 1) * positions] = jnp.sum(
                product[part], axis=0, keepdims=True
            )

    for which in range(count):

        @pl.when(distance == which)
        def _():
            out_refs[which][0] = out_now[...]

    @pl.when(step == count * slots - 1)
    def _():
        pack_all(
            info,
            first_bit(count, slots),
            count,
            info[slots],
            mine_ref,
            send_ref,
            (acc_gate, acc_up, acc_down, acc_out),
        )


def rotate_back(value, cos, sin, heads):
    parts = []
    for head in range(heads):
        low = head * HEAD_DIM
        lead, trail = value[low : low + HALF], value[low + HALF : low + HEAD_DIM]
        parts += [lead * cos + trail * sin, trail * cos - lead * sin]
    return jnp.concatenate(parts, 0)


def attend_back(positions, count, info, *refs):
    q_ref, kv_ref, gattn_ref, log_ref, delta_ref, cos_ref, sin_ref = refs[:7]
    lin_ref, dq, dkv = refs[7:]
    blocks = lax.div(info[pl.program_id(0)] + positions - 1, positions)

    def visit(block, other, diagonal):
        if diagonal:
            mask = causal_mask(positions, GROUPS)
        for group in range(KV_HEADS):
            low = group * HEAD_DIM
            key = kv_ref[0, other, low : low + HEAD_DIM]
            value = kv_ref[0, other, KV_WIDTH + low : KV_WIDTH + low + HEAD_DIM]
            query = heads_side_by_side(q_ref, block, group)
            grad = heads_side_by_side(gattn_ref, block, group)
            scores = dot(key, query, TN)
            probs = jnp.exp(scores - log_ref[0, block, group : group + 1])
            if diagonal:
                probs = jnp.where(mask, probs, 0.0)
            grad_probs = dot(value, grad, TN)
            delta = delta_ref[0, block, group : group + 1]
            grad_scores = (probs * (grad_probs - delta)).astype(BF16)
            grad_query = dot(key, grad_scores)
            grad_key = dot(query, grad_scores, NT)
            grad_value = dot(grad, probs.astype(BF16), NT)
            rows = slice(low, low + HEAD_DIM)
            more = slice(KV_WIDTH + low, KV_WIDTH + low + HEAD_DIM)
            if diagonal:
                dq[rows] = grad_query
                dkv[other, rows] = grad_key
                dkv[other, more] = grad_value
            else:
                dq[rows] += grad_query
                dkv[other, rows] += grad_key
                dkv[other, more] += grad_value

    def one_block(block, carry):
        visit(block, block, True)

        def one_pair(other, carry):
            visit(block, other, False)
            return carry

        lax.fori_loop(0, block, one_pair, 0)
        grad = jnp.concatenate(
            [
                dq[
                    (head // GROUPS) * HEAD_DIM : (head // GROUPS + 1) * HEAD_DIM,
                    (head % GROUPS) * positions : (head % GROUPS + 1) * positions,
                ]
                for head in range(HEADS)
            ],
            0,
        ) * (HEAD_DIM**-0.5)
        lin = rotate_back(grad, cos_ref[block], sin_ref[block], HEADS)
        lin_ref[0, block, :Q_WIDTH] = lin.astype(BF16)
        return carry

    lax.fori_loop(0, blocks, one_block, 0)

    def one_rotation(block, carry):
        grad = dkv[block]
        rotated = rotate_back(grad[:KV_WIDTH], cos_ref[block], sin_ref[block], KV_HEADS)
        lin_ref[0, block, Q_WIDTH : Q_WIDTH + KV_WIDTH] = rotated.astype(BF16)
        lin_ref[0, block, Q_WIDTH + KV_WIDTH :] = grad[KV_WIDTH:].astype(BF16)
        return carry

    lax.fori_loop(0, blocks, one_rotation, 0)


def project_back(positions, count, slots, info, *refs):
    x_refs, refs = refs[:count], refs[count:]
    gain_ref, normed_ref, lin_ref, mid_ref, w_ref, other_gain_ref = refs[:6]
    out_refs, refs = refs[6 : 6 + count], refs[6 + count :]
    mine_ref, send_ref, gain_sum, acc_q, acc_k, acc_v, x_now, out_now = refs
    step = pl.program_id(0)
    distance, slot = lax.div(step, slots), lax.rem(step, slots)
    blk = info[slots]
    rows = valid_rows(info, slot, blk ^ distance, positions)

    @pl.when(step == 0)
    def _():
        acc_q[...] = jnp.zeros_like(acc_q)
        acc_k[...] = jnp.zeros_like(acc_k)
        acc_v[...] = jnp.zeros_like(acc_v)
        gain_sum[...] = jnp.zeros_like(gain_sum)

    for which in range(count):

        @pl.when(jnp.logical_and(rows > 0, distance == which))
        def _():
            x_now[...] = x_refs[which][0]

    @pl.when(rows <= 0)
    def _():
        out_now[...] = jnp.zeros_like(out_now)

    @pl.when(rows > 0)
    def _():
        lin = lin_ref[0, 0]
        normed = normed_ref[0, 0]
        acc_q[...] += dot(normed, lin[:Q_WIDTH], NT)
        acc_k[...] += dot(lin[Q_WIDTH : Q_WIDTH + KV_WIDTH], normed, NT)
        acc_v[...] += dot(lin[Q_WIDTH + KV_WIDTH :], normed, NT)
        grad_normed = dot(w_ref[...], lin)
        x = x_now[...].astype(F32)
        scaled = lax.rsqrt(jnp.mean(x * x, axis=0, keepdims=True) + EPS)
        normal = x * scaled
        gain_sum[...] += grad_normed * normal
        inner = grad_normed * gain_ref[...]
        mean = jnp.mean(inner * normal, axis=0, keepdims=True)
        middle = mid_ref[0, 0].astype(F32)
        out_now[...] = (middle + scaled * (inner - normal * mean)).astype(BF16)

    for which in range(count):

        @pl.when(distance == which)
        def _():
            out_refs[which][0] = out_now[...]

    @pl.when(step == count * slots - 1)
    def _():
        gains = gain_rows(gain_sum) + gain_rows(other_gain_ref)
        gains.append(jnp.zeros((-len(gains) % 16, LANES), F32))
        gains = jnp.concatenate(gains, 0).astype(BF16)
        pack_all(
            info,
            first_bit(count, slots),
            count,
            blk,
            mine_ref,
            send_ref,
            (acc_q, acc_k, acc_v),
            gains,
        )


def unpack(count, slots, shapes, gain_width, start, size, info, *refs):
    out_refs, buffer = refs[2 * count : -1], refs[-1]
    core = info[first_bit(count, slots)]
    for which in range(2):
        for distance in range(count):
            part = (core ^ which) * count + (info[slots] ^ distance)
            buffer[pl.ds(pl.multiple_of(part * size, 16), size)] = refs[which * count + distance][
                start : start + size
            ]
    row = 0
    for ref, (rows, columns) in zip(out_refs, shapes):
        for first, width in pieces_of(columns):
            if width == LANES:
                ref[:, first : first + LANES] = buffer[row : row + rows].astype(F32)
                row += rows
            else:
                half = rows // 2
                part = buffer[row : row + half].astype(F32)
                ref[:half, first : first + width] = part[:, :width]
                ref[half:, first : first + width] = part[:, width:]
                row += half
    if gain_width:
        gains = buffer[row : row + 16].astype(F32)
        line = 0
        for ref in out_refs[len(shapes) :]:
            for first, width in pieces_of(gain_width):
                ref[:, first : first + width] = gains[line : line + 1, :width]
                line += 1


def line_up(count, at, info, *refs):
    size = refs[0].shape[0]
    for distance in range(count):
        start = pl.multiple_of((info[at] ^ distance) * size, 16)
        refs[count][pl.ds(start, size)] = refs[distance][...]


def added(arrays):
    total = arrays[0].astype(F32)
    for array in arrays[1:]:
        total = total + array.astype(F32)
    return total.astype(BF16)


class Sum:
    def __init__(self, blk_count, batch_count):
        self.blk_count, self.rest_count = blk_count, batch_count // 2
        self.rest = lax.axis_index("batch") // 2

    def swap_cores(self, array):
        pairs = [(i, i ^ 1) for i in range(2 * self.rest_count)]
        return lax.ppermute(array, "batch", pairs)

    def over_blk(self, array, distance):
        return lax.ppermute(array, "blk", [(i, i ^ distance) for i in range(self.blk_count)])

    def over_rest(self, array, distance):
        pairs = [(i, i ^ (2 * distance)) for i in range(2 * self.rest_count)]
        return lax.ppermute(array, "batch", pairs)

    def reduce_blk(self, mine, send):
        got = self.swap_cores(send)
        size = mine.shape[0] // self.blk_count
        parts = []
        for distance in range(self.blk_count):
            rows = slice(distance * size, (distance + 1) * size)
            parts.append(added([mine[rows], got[rows]]))
        return [parts[0]] + [self.over_blk(parts[d], d) for d in range(1, self.blk_count)]

    def reduce_rest(self, arrays):
        size = arrays[0].shape[0] // self.rest_count
        shares = []
        for distance in range(self.rest_count):
            start = (self.rest ^ distance) * size
            shares.append(added([lax.dynamic_slice_in_dim(a, start, size, 0) for a in arrays]))
        got = [self.over_rest(shares[d], d) for d in range(1, self.rest_count)]
        share = added([shares[0]] + got)
        return [share] + [self.over_rest(share, d) for d in range(1, self.rest_count)]

    def reduce_rest_small(self, arrays):
        piece = added(arrays)
        return added([piece] + [self.over_rest(piece, d) for d in range(1, self.rest_count)])

    def gather_blk(self, piece):
        own = [piece] + [self.over_blk(piece, d) for d in range(1, self.blk_count)]
        return own, [self.swap_cores(part) for part in own]


def on_device(
    blk_count,
    batch_count,
    hidden_in,
    lengths,
    attn_gain,
    w_query,
    w_key,
    w_value,
    w_output,
    mlp_gain,
    w_gate,
    w_up,
    w_down,
    cotangent,
):
    seqs, positions, width = hidden_in.shape
    ff = w_gate.shape[1]
    count = blk_count
    devices = blk_count * batch_count
    slots = -(-seqs // count)
    wide = GROUPS * positions
    blk = lax.axis_index("blk")
    x_t = jnp.swapaxes(hidden_in, 1, 2)
    cot_t = jnp.swapaxes(cotangent, 1, 2)

    numbers = jnp.arange(seqs, dtype=jnp.int32)
    ahead = (lengths[None, :] > lengths[:, None]) | (
        (lengths[None, :] == lengths[:, None]) & (numbers[None, :] < numbers[:, None])
    )
    rank = jnp.sum(ahead.astype(jnp.int32), 1)
    slot_of, place = rank // count, rank % count
    owner = jnp.where(slot_of % 2 == 0, place, count - 1 - place)
    wanted_device = blk ^ jnp.repeat(jnp.arange(count, dtype=jnp.int32), slots)
    wanted_slot = jnp.tile(jnp.arange(slots, dtype=jnp.int32), count)
    match = (
        (owner[None, :] == wanted_device[:, None]) & (slot_of[None, :] == wanted_slot[:, None])
    ).astype(jnp.int32)
    sequence = jnp.sum(match * numbers[None, :], 1)
    own_lengths = jnp.sum(match[:slots] * lengths[None, :], 1)
    batch = lax.axis_index("batch")
    info = jnp.concatenate(
        [own_lengths, jnp.stack([blk]), sequence, jnp.stack([batch % 2, batch // 2])]
        + [owner ^ blk, slot_of]
    ).astype(jnp.int32)
    bit_at = first_bit(count, slots)
    total = Sum(blk_count, batch_count)

    frequency = np.float32(THETA) ** (
        -np.arange(HALF, dtype=np.float32) * np.float32(2.0) / np.float32(HEAD_DIM)
    )
    places = np.arange(count * positions, dtype=np.float32).reshape(count, 1, positions)
    angles = (frequency[None, :, None] * places).astype(np.float32)
    cos_table, sin_table = jnp.asarray(np.cos(angles)), jnp.asarray(np.sin(angles))
    gain_first = attn_gain.astype(F32)[:, None]
    gain_second = mlp_gain.astype(F32)[:, None]
    moved = jax.ShapeDtypeStruct((slots, width, positions), BF16)

    def spread(array, name):
        def source(distance):
            return pl.BlockSpec(
                (1, width, positions),
                lambda slot, info: (info[slots + 1 + distance * slots + slot], 0, 0),
            )

        picked = call(
            functools.partial(pick, count),
            name,
            (slots,),
            [source(distance) for distance in range(count)],
            [per_step(width, positions)] * count,
            [moved] * count,
        )(info, *[array] * count)
        got = [picked[0]]
        for distance in range(1, count):
            pairs = [(i, i ^ distance) for i in range(count)]
            got.append(lax.ppermute(picked[distance], "blk", pairs))
        return got

    def collect(parts, name):
        got = [parts[0]]
        for distance in range(1, count):
            pairs = [(i, i ^ distance) for i in range(count)]
            got.append(lax.ppermute(parts[distance], "blk", pairs))
        last = bit_at + 2

        def source(which):
            def where(seq, info):
                mine = info[last + seq] == which
                return (jnp.where(mine, info[last + seqs + seq], 0), 0, 0)

            return pl.BlockSpec((1, width, positions), where)

        return call(
            functools.partial(put, count, last),
            name,
            (seqs,),
            [source(distance) for distance in range(count)],
            per_step(width, positions),
            jax.ShapeDtypeStruct((seqs, width, positions), BF16),
        )(info, *got)

    x_moved = spread(x_t, "pick_hidden")
    cot_moved = spread(cot_t, "pick_cotangent")

    table = whole(count, HALF, positions)
    blocks_of = lambda rows: per_step(count, rows, positions)
    unit_flops = 4 * slots * count * positions * positions * HEADS * 256
    dense = 2 * slots * count * positions * width
    normed, queries, kv, mix, log_total = call(
        functools.partial(front, positions, count),
        "front",
        (slots,),
        [per_step(width, positions)] * count
        + [whole(width, 1), whole(Q_WIDTH, width), whole(2 * KV_WIDTH, width), table, table],
        [
            blocks_of(width),
            blocks_of(Q_WIDTH),
            blocks_of(2 * KV_WIDTH),
            blocks_of(Q_WIDTH),
            per_step(count, KV_HEADS, wide),
        ],
        [
            jax.ShapeDtypeStruct((slots, count, width, positions), BF16),
            jax.ShapeDtypeStruct((slots, count, Q_WIDTH, positions), BF16),
            jax.ShapeDtypeStruct((slots, count, 2 * KV_WIDTH, positions), BF16),
            jax.ShapeDtypeStruct((slots, count, Q_WIDTH, positions), BF16),
            jax.ShapeDtypeStruct((slots, count, KV_HEADS, wide), F32),
        ],
        [pltpu.VMEM((2 * KV_HEADS, wide), F32), pltpu.VMEM((KV_WIDTH, wide), F32)],
        flops=dense * 960 + 2 * unit_flops,
    )(
        info,
        *x_moved,
        gain_first,
        w_query.T,
        jnp.concatenate([w_key.T, w_value.T], 0),
        cos_table,
        sin_table,
    )

    first_shapes = [(width, ff), (width, ff), (width, ff), (Q_WIDTH, width)]
    first_rows = sum(packed_rows(*shape) for shape in first_shapes)
    unit = 16 * devices
    first_half = -(-first_rows // unit) * unit // 2

    def arrived(distance):
        def where(step, info):
            now = lax.div(step, slots)
            slot = jnp.where(now < distance, 0, slots - 1)
            return (jnp.where(now == distance, lax.rem(step, slots), slot), 0, 0)

        return pl.BlockSpec((1, width, positions), where)

    def block_spec(*shape):
        zeros = (0,) * len(shape)

        def where(step, info):
            return (lax.rem(step, slots), info[slots] ^ lax.div(step, slots)) + zeros

        return pl.BlockSpec((1, 1) + shape, where)

    arrivals = [arrived(distance) for distance in range(count)]
    *layer_t, grad_middle, grad_attn, deltas, mine_first, send_first, gain_sum = call(
        functools.partial(feed_forward, positions, 512, count, slots),
        "feed_forward",
        (slots * count,),
        arrivals * 2
        + [
            block_spec(Q_WIDTH, positions),
            whole(width, 1),
            whole(width, Q_WIDTH),
            whole(Q_WIDTH, width),
            whole(ff, width),
            whole(width, ff),
            whole(ff, width),
            whole(width, ff),
            whole(width, ff),
            whole(ff, width),
        ],
        arrivals
        + [
            block_spec(width, positions),
            block_spec(Q_WIDTH, positions),
            block_spec(KV_HEADS, wide),
            kept(first_half, LANES),
            kept(first_half, LANES),
            kept(width, positions),
        ],
        [moved] * count
        + [
            jax.ShapeDtypeStruct((slots, count, width, positions), BF16),
            jax.ShapeDtypeStruct((slots, count, Q_WIDTH, positions), BF16),
            jax.ShapeDtypeStruct((slots, count, KV_HEADS, wide), F32),
            jax.ShapeDtypeStruct((first_half, LANES), BF16),
            jax.ShapeDtypeStruct((first_half, LANES), BF16),
            jax.ShapeDtypeStruct((width, positions), F32),
        ],
        [pltpu.VMEM(shape, F32) for shape in first_shapes]
        + [pltpu.VMEM((width, positions), BF16)] * 3,
        flops=9 * dense * ff,
    )(
        info,
        *x_moved,
        *cot_moved,
        mix,
        gain_second,
        w_output.T,
        w_output,
        w_gate.T,
        w_gate,
        w_up.T,
        w_up,
        w_down.T,
        w_down,
    )

    parts_first = total.reduce_blk(mine_first, send_first)

    second_shapes = [(width, Q_WIDTH), (KV_WIDTH, width), (KV_WIDTH, width)]
    second_rows = sum(packed_rows(*shape) for shape in second_shapes)
    second_rows += -(-2 * len(pieces_of(width)) // 16) * 16
    second_half = -(-second_rows // unit) * unit // 2
    lin_width = Q_WIDTH + 2 * KV_WIDTH
    grad_lin = call(
        functools.partial(attend_back, positions, count),
        "attend_back",
        (slots,),
        [
            blocks_of(Q_WIDTH),
            blocks_of(2 * KV_WIDTH),
            blocks_of(Q_WIDTH),
            per_step(count, KV_HEADS, wide),
            per_step(count, KV_HEADS, wide),
            table,
            table,
        ],
        blocks_of(lin_width),
        jax.ShapeDtypeStruct((slots, count, lin_width, positions), BF16),
        [
            pltpu.VMEM((KV_WIDTH, wide), F32),
            pltpu.VMEM((count, 2 * KV_WIDTH, positions), F32),
        ],
        flops=5 * unit_flops,
        after=[parts_first[0]],
    )(info, queries, kv, grad_attn, log_total, deltas, cos_table, sin_table)

    *grad_in_t, mine_second, send_second = call(
        functools.partial(project_back, positions, count, slots),
        "project_back",
        (slots * count,),
        arrivals
        + [
            whole(width, 1),
            block_spec(width, positions),
            block_spec(lin_width, positions),
            block_spec(width, positions),
            whole(width, lin_width),
            whole(width, positions),
        ],
        arrivals + [kept(second_half, LANES), kept(second_half, LANES)],
        [moved] * count
        + [
            jax.ShapeDtypeStruct((second_half, LANES), BF16),
            jax.ShapeDtypeStruct((second_half, LANES), BF16),
        ],
        [
            pltpu.VMEM((width, positions), F32),
            pltpu.VMEM((width, Q_WIDTH), F32),
            pltpu.VMEM((KV_WIDTH, width), F32),
            pltpu.VMEM((KV_WIDTH, width), F32),
        ]
        + [pltpu.VMEM((width, positions), BF16)] * 2,
        flops=2 * dense * 960,
        after=parts_first[1:],
    )(
        info,
        *x_moved,
        gain_first,
        normed,
        grad_lin,
        grad_middle,
        jnp.concatenate([w_query, w_key, w_value], 1),
        gain_sum,
    )
    layer_out = collect(layer_t, "put_layer")
    grad_in = collect(grad_in_t, "put_grad")

    shares = total.reduce_rest(parts_first)
    share_rows = shares[0].shape[0]
    rest_count = batch_count // 2
    piece_first = call(
        functools.partial(line_up, rest_count, bit_at + 1),
        "line_up",
        (1,),
        [whole(share_rows, LANES)] * rest_count,
        whole(rest_count * share_rows, LANES),
        jax.ShapeDtypeStruct((rest_count * share_rows, LANES), BF16),
        after=[layer_out, grad_in],
    )(info, *shares)
    piece_second = total.reduce_rest_small(total.reduce_blk(mine_second, send_second))
    own, other = total.gather_blk(jnp.concatenate([piece_first, piece_second], 0))
    size_first, size_second = piece_first.shape[0], piece_second.shape[0]

    def open_up(shapes, gain_width, start, size, name):
        outs = list(shapes) + ([(1, gain_width)] * 2 if gain_width else [])
        return call(
            functools.partial(unpack, count, slots, shapes, gain_width, start, size),
            name,
            (1,),
            [whole(*own[0].shape)] * (2 * count),
            [whole(*shape) for shape in outs],
            [jax.ShapeDtypeStruct(shape, F32) for shape in outs],
            [pltpu.VMEM((2 * count * size, LANES), BF16)],
            bytes_accessed=12 * count * size * LANES,
        )(info, *own, *other)

    g_gate, g_up, g_down_t, g_out = open_up(first_shapes, 0, 0, size_first, "unpack_first")
    g_query, g_key_t, g_value_t, gain_one, gain_two = open_up(
        second_shapes, width, size_first, size_second, "unpack_second"
    )
    return (
        jnp.swapaxes(layer_out, 1, 2),
        jnp.swapaxes(grad_in, 1, 2),
        gain_one.reshape(width),
        g_query,
        g_key_t.T,
        g_value_t.T,
        g_out,
        gain_two.reshape(width),
        g_gate,
        g_up,
        g_down_t.T,
    )


def solution(mesh):
    rows = P("batch", "blk", None)
    return jax.shard_map(
        functools.partial(on_device, mesh.shape["blk"], mesh.shape["batch"]),
        mesh=mesh,
        in_specs=(rows, P("batch")) + (P(),) * 9 + (rows,),
        out_specs=(rows, rows) + (P(),) * 9,
        check_vma=False,
    )
```

time: 838 us -> 368 us (0.44)
  local copies, waits for them, and re-layouts: 253 us -> 17 us
  waiting for transfers between devices: 334 us -> 116 us
  Pallas kernels: 0 us -> 137 us
  matrix products: 128 us -> 0 us
  starting transfers between devices: 0.65 us -> 77.3 us
  blocking collectives: 40.5 us -> 0 us
  other arithmetic: 40.6 us -> 16.8 us
  loops' own time: 18.6 us -> 0 us
  between operations: 14.6 us -> 1 us
    psum x1 -> x0, waiting for transfers between devices: 195 us -> none  [on_device(): lax.psum((grad_attn_gain, grad_w_query, grad_w_key, grad_w_value, grad_w_...]
    pallas_call x0 -> x11, Pallas kernels: none -> 137 us  [call(): return lambda *operands: made(*operands, *after)]
    dot_general x63 -> x0, matrix products: 128 us -> none  [the longest x1 16.6 us: on_device(): jnp.einsum('rd,fd->rf', grad_branch, w_down, preferred_element_type=jnp.f...]
    ppermute x0 -> x36, waiting for transfers between devices: none -> 116 us  [the longest x9 81.7 us: over_blk(): lax.ppermute(array, 'blk', [(i, i ^ distance) for i in range(self.blk_cou...]
    dynamic_update_slice x30 -> x0, local copies, waits for them, and re-layouts: 110 us -> none  [the longest x18 92.3 us: on_device(): lax.map(attend_one_sequence, (queries, kv_piece, lengths, initial[0], ini...]
    reduce_scatter x1 -> x0, waiting for transfers between devices: 84.5 us -> none  [on_device(): lax.psum_scatter(grad_kv.astype(jnp.bfloat16), 'blk', scatter_dimension=1...]
    ppermute x0 -> x36, starting transfers between devices: none -> 77.3 us  [the longest x9 34.6 us: over_rest(): return lax.ppermute(array, 'batch', pairs)]
    all_gather x1 -> x0, waiting for transfers between devices: 54.4 us -> none  [on_device(): kv_piece = lax.all_gather(packed, 'blk', axis=1, tiled=True)]
  transfers between devices with their start and end apart: 3 -> 36, of which waited for: 3 -> 12; matrix products, arithmetic and copies ran while one was open for 8% -> 7% of each run, Pallas kernels for 0% -> 21%
where the time goes in v1:
time: 368 us; the launch traced here: 366 us
  Pallas kernels  137 us (37%)
  waiting for transfers between devices  116 us (32%)
  starting transfers between devices  77.3 us (21%)
  local copies, waits for them, and re-layouts  17 us (5%)
  other arithmetic  16.8 us (5%)
    pallas_call x11, Pallas kernels, call(): return lambda *operands: made(*operands, *after)  137 us
    ppermute x9, waiting for transfers between devices, over_blk(): lax.ppermute(array, 'blk', [(i, i ^ distance) for i in range(self.blk_cou...  81.7 us
    ppermute x9, starting transfers between devices, over_rest(): return lax.ppermute(array, 'batch', pairs)  34.6 us
    ppermute x6, starting transfers between devices, collect(): got.append(lax.ppermute(parts[distance], 'blk', pairs))  23.1 us
    unnamed x71, local copies, waits for them, and re-layouts  14.5 us
    ppermute x9, waiting for transfers between devices, over_rest(): return lax.ppermute(array, 'batch', pairs)  14.5 us
    ppermute x6, waiting for transfers between devices, spread(): got.append(lax.ppermute(picked[distance], 'blk', pairs))  11.1 us
    ppermute x9, starting transfers between devices, over_blk(): lax.ppermute(array, 'blk', [(i, i ^ distance) for i in range(self.blk_cou...  11 us
  transfers between devices with their start and end apart: 36, of which 12 were waited for; matrix products, arithmetic and copies ran while one was open for 7% of the time, Pallas kernels for 21%

profile of v1, /device:TPU:0, one launch (start us, length us, event | category | flops | bytes accessed | tf_op | source)
XLA Modules:
  0.0 365.7 jit_solution(12895109835750759011)
XLA Ops:
  3.4 3.7 %pick_hidden.1 = (bf16[2,576,256]{2,1,0:T(8,128)(2,1)}, bf16[2,576,256]{2,1,0:T(8,128)(2,1)}, bf16[2,576,256]{2,1,0:T(8,128)(2,1)}, bf16[2,576,256]{2,1,0:T(8,128)(2,1)}) custom-call(s32[25]{0:T(128)} %concatenate.12.info, bf16[6,576,256]{2,1,0:T(8,128)(2,1)} %bitcast.17, bf16[6,576,256]{2,1,0:T(8,128)(2,1)} %bitcast.18, bf16[6,576,256]{2,1,0:T(8,128)(2,1)} %bitcast.19, ...), custom_call_target="tpu_custom_call" | custom-call | tf_op jit(solution)/shard_map/pick_hidden/pallas_call | solution.py:62
  7.1 2.9 collective-permute-start
  10.0 1.5 collective-permute-start.1
  11.6 3.9 %pick_cotangent.1 = (bf16[2,576,256]{2,1,0:T(8,128)(2,1)}, bf16[2,576,256]{2,1,0:T(8,128)(2,1)}, bf16[2,576,256]{2,1,0:T(8,128)(2,1)}, bf16[2,576,256]{2,1,0:T(8,128)(2,1)}) custom-call(s32[25]{0:T(128)} %concatenate.12.info, bf16[6,576,256]{2,1,0:T(8,128)(2,1)} %bitcast.21, bf16[6,576,256]{2,1,0:T(8,128)(2,1)} %bitcast.22, bf16[6,576,256]{2,1,0:T(8,128)(2,1)} %bitcast.23, ...), custom_call_target="tpu_custom_call" | custom-call | tf_op jit(solution)/shard_map/pick_cotangent/pallas_call | solution.py:62
  15.5 2.0 collective-permute-start.3
  17.5 1.5 collective-permute-start.4
  21.1 2.3 copy.46
  23.3 2.3 copy.45
  25.6 2.3 copy.48.refs_17_
  30.8 8.5 %collective-permute-done.1.refs_2_ = bf16[2,576,256]{2,1,0:T(8,128)(2,1)} collective-permute-done((bf16[2,576,256]{2,1,0:T(8,128)(2,1)}, bf16[2,576,256]{2,1,0:T(8,128)(2,1)}, u32[]{:S(2)}, u32[]{:S(2)}) %collective-permute-start.1) | collective-permute-done | bytes 589856 | tf_op jit(solution)/shard_map/ppermute | solution.py:715
  39.3 21.3 %front.1 = (bf16[2,4,576,256]{3,2,1,0:T(8,128)(2,1)}, bf16[2,4,576,256]{3,2,1,0:T(8,128)(2,1)}, bf16[2,4,384,256]{3,2,1,0:T(8,128)(2,1)}, bf16[2,4,576,256]{3,2,1,0:T(8,128)(2,1)}, f32[2,4,3,768]{3,2,1,0:T(4,128)}) custom-call(s32[25]{0:T(128)} %concatenate.12.info, bf16[2,576,256]{2,1,0:T(8,128)(2,1)} %get-tuple-element.49.refs_0_, ...), custom_call_target="tpu_custom_call" | custom-call | flops 11928600576 | tf_op jit(solution)/shard_map/front/pallas_call | solution.py:62
  60.5 2.6 collective-permute-done.4.refs_6_
  63.9 42.1 %feed_forward.1 = (bf16[2,576,256]{2,1,0:T(8,128)(2,1)}, bf16[2,576,256]{2,1,0:T(8,128)(2,1)}, bf16[2,576,256]{2,1,0:T(8,128)(2,1)}, bf16[2,576,256]{2,1,0:T(8,1...) custom-call(s32[25]{0:T(128)} %concatenate.12.info, ...), custom_call_target="tpu_custom_call" | custom-call | flops 32614907904 | tf_op jit(solution)/shard_map/feed_forward/pallas_call | solution.py:62
  106.3 2.0 copy.50
  108.2 2.5 pad_maximum_fusion.refs_8_
  111.9 13.8 %collective-permute-start.7 = (bf16[2,576,256]{2,1,0:T(8,128)(2,1)}, bf16[2,576,256]{2,1,0:T(8,128)(2,1)}, u32[]{:S(2)}, u32[]{:S(2)}) collective-permute-start(bf16[2,576,256]{2,1,0:T(8,128)(2,1)} %get-tuple-element.60), channel_id=1, source_target_pairs={{0,16},{8,24},{16,0},{24,8},{1,17},{9,25},{17,1},{25,9},{2,18},{10... | collective-permute-start | bytes 1769480 | tf_op jit(solution)/shard_map/ppermute | solution.py:722
  125.7 3.9 %add_convert_fusion = (bf16[2944,128]{1,0:T(8,128)(2,1)}, bf16[2944,128]{1,0:T(8,128)(2,1)}, bf16[2944,128]{1,0:T(8,128)(2,1)}, bf16[2944,128]{1,0:T(8,128)(2,1)}) fusion(bf16[11776,128]{1,0:T(8,128)(2,1)} %collective-permute-done.9, bf16[11776,128]{1,0:T(8,128)(2,1)S(1)} %copy-done.7), kind=kLoop, calls=%fused_computation | loop fusion | flops 6029312 | bytes 9043968 | tf_op jit(solution)/shard_map/convert_element_type | solution.py:592
  129.6 2.0 collective-permute-start.10
  131.7 1.5 collective-permute-start.12
  133.1 24.5 %attend_back.1.refs_6_ = bf16[2,4,960,256]{3,2,1,0:T(8,128)(2,1)} custom-call(s32[25]{0:T(128)} %concatenate.12.info, bf16[2,4,576,256]{3,2,1,0:T(8,128)(2,1)} %get-tuple-element.63.refs_0_, bf16[2,4,384,256]{3,2,1,0:T(8,128)(2,1)} %get-tuple-element.64.refs_1_, bf16[2,4,576,256]{3,2,1,0:T(8,128)(2,1)} %get-tuple-element.65.refs_2_, ...), custom_call_target="tpu_custom_call" | custom-call | flops 24159191040 | tf_op jit(solution)/shard_map/attend_back/pallas_call | solution.py:62
  157.7 13.8 %collective-permute-done.11.refs_11_ = bf16[2944,128]{1,0:T(8,128)(2,1)S(1)} collective-permute-done((bf16[2944,128]{1,0:T(8,128)(2,1)}, bf16[2944,128]{1,0:T(8,128)(2,1)S(1)}, u32[]{:S(2)}, u32[]{:S(2)}) %collective-permute-start.11) | collective-permute-done | bytes 753696 | tf_op jit(solution)/shard_map/ppermute | solution.py:605
  171.5 1.8 collective-permute-done.12.refs_12_
  173.6 18.6 %collective-permute-start.16 = (bf16[736,128]{1,0:T(8,128)(2,1)S(1)}, bf16[736,128]{1,0:T(8,128)(2,1)S(1)}, u32[]{:S(2)}, u32[]{:S(2)}) collective-permute-start(bf16[736,128]{1,0:T(8,128)(2,1)S(1)} %get-tuple-element.96), channel_id=1, source_target_pairs={{0,2},{1,3},{2,0},{3,1},{4,6},{5,7},{6,4},{7,5},{8,10},{9,11},{10,... | collective-permute-start | bytes 565256 | tf_op jit(solution)/shard_map/ppermute | solution.py:609
  192.3 14.2 %project_back.1 = (bf16[2,576,256]{2,1,0:T(8,128)(2,1)}, bf16[2,576,256]{2,1,0:T(8,128)(2,1)}, bf16[2,576,256]{2,1,0:T(8,128)(2,1)}, bf16[2,576,256]{2,1,0:T(8,1...) custom-call(s32[25]{0:T(128)} %concatenate.12.info, bf16[2,576,256]{2,1,0:T(8,128)(2,1)} %get-tuple-element.49.refs_0_, ...), custom_call_target="tpu_custom_call" | custom-call | flops 4529848320 | tf_op jit(solution)/shard_map/project_back/pallas_call | solution.py:62
  206.6 6.4 %collective-permute-start.17 = (bf16[736,128]{1,0:T(8,128)(2,1)S(1)}, bf16[736,128]{1,0:T(8,128)(2,1)S(1)}, u32[]{:S(2)}, u32[]{:S(2)}) collective-permute-start(bf16[736,128]{1,0:T(8,128)(2,1)S(1)} %get-tuple-element.98), channel_id=1, source_target_pairs={{0,4},{1,5},{2,6},{3,7},{4,0},{5,1},{6,2},{7,3},{8,12},{9,13},{10,... | collective-permute-start | bytes 565256 | tf_op jit(solution)/shard_map/ppermute | solution.py:609
  213.2 13.4 %collective-permute-done.17 = bf16[736,128]{1,0:T(8,128)(2,1)S(1)} collective-permute-done((bf16[736,128]{1,0:T(8,128)(2,1)S(1)}, bf16[736,128]{1,0:T(8,128)(2,1)S(1)}, u32[]{:S(2)}, u32[]{:S(2)}) %collective-permute-start.17) | collective-permute-done | bytes 188448 | tf_op jit(solution)/shard_map/ppermute | solution.py:609
  226.6 4.6 %collective-permute-start.8 = (bf16[2,576,256]{2,1,0:T(8,128)(2,1)}, bf16[2,576,256]{2,1,0:T(8,128)(2,1)S(1)}, u32[]{:S(2)}, u32[]{:S(2)}) collective-permute-start(bf16[2,576,256]{2,1,0:T(8,128)(2,1)} %get-tuple-element.61), channel_id=1, source_target_pairs={{0,24},{8,16},{16,8},{24,0},{1,25},{9,17},{17,9},{25,1},{2,26},{10... | collective-permute-start | bytes 1769480 | tf_op jit(solution)/shard_map/ppermute | solution.py:722
  231.3 1.3 add_convert_fusion.4.refs_0_
  233.1 2.9 collective-permute-start.15
  236.1 1.7 collective-permute-start.19
  238.9 6.7 %collective-permute-done.8.refs_3_ = bf16[2,576,256]{2,1,0:T(8,128)(2,1)S(1)} collective-permute-done((bf16[2,576,256]{2,1,0:T(8,128)(2,1)}, bf16[2,576,256]{2,1,0:T(8,128)(2,1)S(1)}, u32[]{:S(2)}, u32[]{:S(2)}) %collective-permute-start.8) | collective-permute-done | bytes 589856 | tf_op jit(solution)/shard_map/ppermute | solution.py:722
  245.7 3.4 collective-permute-start.24
  249.2 23.6 %collective-permute-done.23 = bf16[576,128]{1,0:T(8,128)(2,1)S(1)} collective-permute-done((bf16[576,128]{1,0:T(8,128)(2,1)S(1)}, bf16[576,128]{1,0:T(8,128)(2,1)S(1)}, u32[]{:S(2)}, u32[]{:S(2)}) %collective-permute-start.23) | collective-permute-done | bytes 147488 | tf_op jit(solution)/shard_map/ppermute | solution.py:605
  273.1 5.8 %collective-permute-done.25 = bf16[576,128]{1,0:T(8,128)(2,1)S(1)} collective-permute-done((bf16[576,128]{1,0:T(8,128)(2,1)S(1)}, bf16[576,128]{1,0:T(8,128)(2,1)S(1)}, u32[]{:S(2)}, u32[]{:S(2)}) %collective-permute-start.25) | collective-permute-done | bytes 147488 | tf_op jit(solution)/shard_map/ppermute | solution.py:605
  278.9 3.2 collective-permute-start.21
  284.4 3.2 collective-permute-start.28
  287.6 5.2 %put_layer.1.refs_4_ = bf16[6,576,256]{2,1,0:T(8,128)(2,1)} custom-call(s32[25]{0:T(128)} %concatenate.12.info, bf16[2,576,256]{2,1,0:T(8,128)(2,1)} %get-tuple-element.58.refs_0_, bf16[2,576,256]{2,1,0:T(8,128)(2,1)} %collective-permute-done.6.refs_1_, bf16[2,576,256]{2,1,0:T(8,128)(2,1)} %collective-permute-done.7.refs_2_, bf16[2,576,256]{2,1,0:T(8,128)(2,1)} %copy-done.20), custom_call_target="tpu_custom_call" | custom-call | tf_op jit(solution)/shard_map/put_layer/pallas_call | solution.py:62
  292.9 5.2 %put_grad.1.refs_5_ = bf16[6,576,256]{2,1,0:T(8,128)(2,1)} custom-call(s32[25]{0:T(128)} %concatenate.12.info, bf16[2,576,256]{2,1,0:T(8,128)(2,1)} %get-tuple-element.72.refs_0_, bf16[2,576,256]{2,1,0:T(8,128)(2,1)} %copy-done.21, bf16[2,576,256]{2,1,0:T(8,128)(2,1)} %copy-done.22, bf16[2,576,256]{2,1,0:T(8,128)(2,1)} %copy-done.23), custom_call_target="tpu_custom_call" | custom-call | tf_op jit(solution)/shard_map/put_grad/pallas_call | solution.py:62
  299.4 2.8 line_up.1
  304.5 1.6 collective-permute-start.29
  306.1 1.7 collective-permute-start.30
  308.2 19.3 %collective-permute-done.29.refs_1_ = bf16[3520,128]{1,0:T(8,128)(2,1)S(1)} collective-permute-done((bf16[3520,128]{1,0:T(8,128)(2,1)S(1)}, bf16[3520,128]{1,0:T(8,128)(2,1)S(1)}, u32[]{:S(2)}, u32[]{:S(2)}) %collective-permute-start.29) | collective-permute-done | bytes 901152 | tf_op jit(solution)/shard_map/ppermute | solution.py:605
  327.5 17.3 %collective-permute-done.30.refs_2_ = bf16[3520,128]{1,0:T(8,128)(2,1)S(1)} collective-permute-done((bf16[3520,128]{1,0:T(8,128)(2,1)S(1)}, bf16[3520,128]{1,0:T(8,128)(2,1)S(1)}, u32[]{:S(2)}, u32[]{:S(2)}) %collective-permute-start.30) | collective-permute-done | bytes 901152 | tf_op jit(solution)/shard_map/ppermute | solution.py:605
  345.4 2.4 collective-permute-done.34.refs_6_
  348.7 5.4 %unpack_second.1 = (f32[576,576]{1,0:T(8,128)}, f32[192,576]{1,0:T(8,128)}, f32[192,576]{1,0:T(8,128)}, f32[1,576]{1,0:T(1,128)}, f32[1,576]{1,0:T(1,128)}) custom-call(s32[25]{0:T(128)} %concatenate.12.info, bf16[3520,128]{1,0:T(8,128)(2,1)} %copy-done, bf16[3520,128]{1,0:T(8,128)(2,1)} %copy-done.1, bf16[3520,128]{1,0:T(8,128)(2,1)} %copy-done.2, ...), custom_call_target="tpu_custom_call" | custom-call | bytes 3538944 | tf_op jit(solution)/shard_map/unpack_second/pallas_call | solution.py:62
  354.1 1.3 reduce
  355.4 1.3 reduce.1
  356.7 9.1 %unpack_first.1 = (f32[576,1536]{1,0:T(8,128)}, f32[576,1536]{1,0:T(8,128)}, f32[576,1536]{1,0:T(8,128)}, f32[576,576]{1,0:T(8,128)}) custom-call(s32[25]{0:T(128)} %concatenate.12.info, bf16[3520,128]{1,0:T(8,128)(2,1)} %copy-done, bf16[3520,128]{1,0:T(8,128)(2,1)} %copy-done.1, bf16[3520,128]{1,0:T(8,128)(2,1)} %copy-done.2, bf16[3520,128]{1,0:T(8,128)(2,1)} %copy-done.3, ...), custom_call_target="tpu_custom_call" | custom-call | bytes 18087936 | tf_op jit(solution)/shard_map/unpack_first/pallas_call | solution.py:62
  (128 shorter events, 20.4 us)
Async XLA Ops:
  7.1 23.6 %collective-permute-start = (bf16[2,576,256]{2,1,0:T(8,128)(2,1)}, bf16[2,576,256]{2,1,0:T(8,128)(2,1)}, u32[]{:S(2)}, u32[]{:S(2)}) collective-permute-start(bf16[2,576,256]{2,1,0:T(8,128)(2,1)} %get-tuple-element.50), channel_id=1, source_target_pairs={{0,8},{8,0},{16,24},{24,16},{1,9},{9,1},{17,25},{25,17},{2,10},{10... | collective-permute-start | bytes 1769480 | tf_op jit(solution)/shard_map/ppermute | solution.py:715
  10.0 29.2 %collective-permute-start.1 = (bf16[2,576,256]{2,1,0:T(8,128)(2,1)}, bf16[2,576,256]{2,1,0:T(8,128)(2,1)}, u32[]{:S(2)}, u32[]{:S(2)}) collective-permute-start(bf16[2,576,256]{2,1,0:T(8,128)(2,1)} %get-tuple-element.51), channel_id=1, source_target_pairs={{0,16},{8,24},{16,0},{24,8},{1,17},{9,25},{17,1},{25,9},{2,18},{10... | collective-permute-start | bytes 1769480 | tf_op jit(solution)/shard_map/ppermute | solution.py:715
  11.6 27.7 %collective-permute-start.2 = (bf16[2,576,256]{2,1,0:T(8,128)(2,1)}, bf16[2,576,256]{2,1,0:T(8,128)(2,1)}, u32[]{:S(2)}, u32[]{:S(2)}) collective-permute-start(bf16[2,576,256]{2,1,0:T(8,128)(2,1)} %get-tuple-element.52), channel_id=1, source_target_pairs={{0,24},{8,16},{16,8},{24,0},{1,25},{9,17},{17,9},{25,1},{2,26},{10... | collective-permute-start | bytes 1769480 | tf_op jit(solution)/shard_map/ppermute | solution.py:715
  15.5 45.0 %collective-permute-start.3 = (bf16[2,576,256]{2,1,0:T(8,128)(2,1)}, bf16[2,576,256]{2,1,0:T(8,128)(2,1)}, u32[]{:S(2)}, u32[]{:S(2)}) collective-permute-start(bf16[2,576,256]{2,1,0:T(8,128)(2,1)} %get-tuple-element.54), channel_id=1, source_target_pairs={{0,8},{8,0},{16,24},{24,16},{1,9},{9,1},{17,25},{25,17},{2,10},{10... | collective-permute-start | bytes 1769480 | tf_op jit(solution)/shard_map/ppermute | solution.py:715
  17.5 45.6 %collective-permute-start.4 = (bf16[2,576,256]{2,1,0:T(8,128)(2,1)}, bf16[2,576,256]{2,1,0:T(8,128)(2,1)}, u32[]{:S(2)}, u32[]{:S(2)}) collective-permute-start(bf16[2,576,256]{2,1,0:T(8,128)(2,1)} %get-tuple-element.55), channel_id=1, source_target_pairs={{0,16},{8,24},{16,0},{24,8},{1,17},{9,25},{17,1},{25,9},{2,18},{10... | collective-permute-start | bytes 1769480 | tf_op jit(solution)/shard_map/ppermute | solution.py:715
  30.7 32.4 %collective-permute-start.5 = (bf16[2,576,256]{2,1,0:T(8,128)(2,1)S(1)}, bf16[2,576,256]{2,1,0:T(8,128)(2,1)S(1)}, u32[]{:S(2)}, u32[]{:S(2)}) collective-permute-start(bf16[2,576,256]{2,1,0:T(8,128)(2,1)S(1)} %copy-done.30), channel_id=1, source_target_pairs={{0,24},{8,16},{16,8},{24,0},{1,25},{9,17},{17,9},{25,1},{2,26},{10... | collective-permute-start | bytes 1769480 | tf_op jit(solution)/shard_map/ppermute | solution.py:715
  106.0 19.7 %collective-permute-start.9 = (bf16[11776,128]{1,0:T(8,128)(2,1)}, bf16[11776,128]{1,0:T(8,128)(2,1)}, u32[]{:S(2)}, u32[]{:S(2)}) collective-permute-start(bf16[11776,128]{1,0:T(8,128)(2,1)} %get-tuple-element.69), channel_id=1, source_target_pairs={{0,1},{1,0},{2,3},{3,2},{4,5},{5,4},{6,7},{7,6},{8,9},{9,8},{10,11... | collective-permute-start | bytes 9043976 | tf_op jit(solution)/shard_map/ppermute | solution.py:602
  106.1 19.6 %copy-start.7 = (bf16[11776,128]{1,0:T(8,128)(2,1)S(1)}, bf16[11776,128]{1,0:T(8,128)(2,1)}, u32[]{:S(2)}) copy-start(bf16[11776,128]{1,0:T(8,128)(2,1)} %get-tuple-element.68) | copy-start | bytes 9043972
  110.7 121.8 %collective-permute-start.6 = (bf16[2,576,256]{2,1,0:T(8,128)(2,1)}, bf16[2,576,256]{2,1,0:T(8,128)(2,1)}, u32[]{:S(2)}, u32[]{:S(2)}) collective-permute-start(bf16[2,576,256]{2,1,0:T(8,128)(2,1)} %get-tuple-element.59), channel_id=1, source_target_pairs={{0,8},{8,0},{16,24},{24,16},{1,9},{9,1},{17,25},{25,17},{2,10},{10... | collective-permute-start | bytes 1769480 | tf_op jit(solution)/shard_map/ppermute | solution.py:722
  111.9 121.3 %collective-permute-start.7 = (bf16[2,576,256]{2,1,0:T(8,128)(2,1)}, bf16[2,576,256]{2,1,0:T(8,128)(2,1)}, u32[]{:S(2)}, u32[]{:S(2)}) collective-permute-start(bf16[2,576,256]{2,1,0:T(8,128)(2,1)} %get-tuple-element.60), channel_id=1, source_target_pairs={{0,16},{8,24},{16,0},{24,8},{1,17},{9,25},{17,1},{25,9},{2,18},{10... | collective-permute-start | bytes 1769480 | tf_op jit(solution)/shard_map/ppermute | solution.py:722
  129.6 28.0 %collective-permute-start.10 = (bf16[2944,128]{1,0:T(8,128)(2,1)}, bf16[2944,128]{1,0:T(8,128)(2,1)S(1)}, u32[]{:S(2)}, u32[]{:S(2)}) collective-permute-start(bf16[2944,128]{1,0:T(8,128)(2,1)} %get-tuple-element.94), channel_id=1, source_target_pairs={{0,8},{8,0},{16,24},{24,16},{1,9},{9,1},{17,25},{25,17},{2,10},{10... | collective-permute-start | bytes 2261000 | tf_op jit(solution)/shard_map/ppermute | solution.py:605
  131.6 39.9 %collective-permute-start.11 = (bf16[2944,128]{1,0:T(8,128)(2,1)}, bf16[2944,128]{1,0:T(8,128)(2,1)S(1)}, u32[]{:S(2)}, u32[]{:S(2)}) collective-permute-start(bf16[2944,128]{1,0:T(8,128)(2,1)} %get-tuple-element.93), channel_id=1, source_target_pairs={{0,16},{8,24},{16,0},{24,8},{1,17},{9,25},{17,1},{25,9},{2,18},{10... | collective-permute-start | bytes 2261000 | tf_op jit(solution)/shard_map/ppermute | solution.py:605
  131.7 41.7 %collective-permute-start.12 = (bf16[2944,128]{1,0:T(8,128)(2,1)}, bf16[2944,128]{1,0:T(8,128)(2,1)S(1)}, u32[]{:S(2)}, u32[]{:S(2)}) collective-permute-start(bf16[2944,128]{1,0:T(8,128)(2,1)} %get-tuple-element.92), channel_id=1, source_target_pairs={{0,24},{8,16},{16,8},{24,0},{1,25},{9,17},{17,9},{25,1},{2,26},{10... | collective-permute-start | bytes 2261000 | tf_op jit(solution)/shard_map/ppermute | solution.py:605
  133.1 40.2 %copy-start.8 = (bf16[2944,128]{1,0:T(8,128)(2,1)S(1)}, bf16[2944,128]{1,0:T(8,128)(2,1)}, u32[]{:S(2)}) copy-start(bf16[2944,128]{1,0:T(8,128)(2,1)} %get-tuple-element.95.refs_7_) | copy-start | bytes 2260996
  157.7 34.6 %copy-start.15 = (bf16[2944,128]{1,0:T(8,128)(2,1)}, bf16[2944,128]{1,0:T(8,128)(2,1)S(1)}, u32[]{:S(2)}) copy-start(bf16[2944,128]{1,0:T(8,128)(2,1)S(1)} %collective-permute-done.10.refs_10_) | copy-start | bytes 2260996
  171.5 20.8 %copy-start.16 = (bf16[2944,128]{1,0:T(8,128)(2,1)}, bf16[2944,128]{1,0:T(8,128)(2,1)S(1)}, u32[]{:S(2)}) copy-start(bf16[2944,128]{1,0:T(8,128)(2,1)S(1)} %collective-permute-done.11.refs_11_) | copy-start | bytes 2260996
  173.3 18.9 %copy-start.17 = (bf16[2944,128]{1,0:T(8,128)(2,1)}, bf16[2944,128]{1,0:T(8,128)(2,1)S(1)}, u32[]{:S(2)}) copy-start(bf16[2944,128]{1,0:T(8,128)(2,1)S(1)} %collective-permute-done.12.refs_12_) | copy-start | bytes 2260996
  173.6 39.4 %collective-permute-start.16 = (bf16[736,128]{1,0:T(8,128)(2,1)S(1)}, bf16[736,128]{1,0:T(8,128)(2,1)S(1)}, u32[]{:S(2)}, u32[]{:S(2)}) collective-permute-start(bf16[736,128]{1,0:T(8,128)(2,1)S(1)} %get-tuple-element.96), channel_id=1, source_target_pairs={{0,2},{1,3},{2,0},{3,1},{4,6},{5,7},{6,4},{7,5},{8,10},{9,11},{10,... | collective-permute-start | bytes 565256 | tf_op jit(solution)/shard_map/ppermute | solution.py:609
  206.5 31.3 %copy-start.24 = (bf16[2304,128]{1,0:T(8,128)(2,1)S(1)}, bf16[2304,128]{1,0:T(8,128)(2,1)}, u32[]{:S(2)}) copy-start(bf16[2304,128]{1,0:T(8,128)(2,1)} %get-tuple-element.76) | copy-start | bytes 1769476
  206.5 29.6 %collective-permute-start.22 = (bf16[2304,128]{1,0:T(8,128)(2,1)}, bf16[2304,128]{1,0:T(8,128)(2,1)}, u32[]{:S(2)}, u32[]{:S(2)}) collective-permute-start(bf16[2304,128]{1,0:T(8,128)(2,1)} %get-tuple-element.77), channel_id=1, source_target_pairs={{0,1},{1,0},{2,3},{3,2},{4,5},{5,4},{6,7},{7,6},{8,9},{9,8},{10,11... | collective-permute-start | bytes 1769480 | tf_op jit(solution)/shard_map/ppermute | solution.py:602
  206.6 20.0 %collective-permute-start.17 = (bf16[736,128]{1,0:T(8,128)(2,1)S(1)}, bf16[736,128]{1,0:T(8,128)(2,1)S(1)}, u32[]{:S(2)}, u32[]{:S(2)}) collective-permute-start(bf16[736,128]{1,0:T(8,128)(2,1)S(1)} %get-tuple-element.98), channel_id=1, source_target_pairs={{0,4},{1,5},{2,6},{3,7},{4,0},{5,1},{6,2},{7,3},{8,12},{9,13},{10,... | collective-permute-start | bytes 565256 | tf_op jit(solution)/shard_map/ppermute | solution.py:609
  213.0 18.2 %collective-permute-start.18 = (bf16[736,128]{1,0:T(8,128)(2,1)S(1)}, bf16[736,128]{1,0:T(8,128)(2,1)S(1)}, u32[]{:S(2)}, u32[]{:S(2)}) collective-permute-start(bf16[736,128]{1,0:T(8,128)(2,1)S(1)} %get-tuple-element.97), channel_id=1, source_target_pairs={{0,6},{1,7},{2,4},{3,5},{4,2},{5,3},{6,0},{7,1},{8,14},{9,15},{10,... | collective-permute-start | bytes 565256 | tf_op jit(solution)/shard_map/ppermute | solution.py:609
  226.6 19.0 %collective-permute-start.8 = (bf16[2,576,256]{2,1,0:T(8,128)(2,1)}, bf16[2,576,256]{2,1,0:T(8,128)(2,1)S(1)}, u32[]{:S(2)}, u32[]{:S(2)}) collective-permute-start(bf16[2,576,256]{2,1,0:T(8,128)(2,1)} %get-tuple-element.61), channel_id=1, source_target_pairs={{0,24},{8,16},{16,8},{24,0},{1,25},{9,17},{17,9},{25,1},{2,26},{10... | collective-permute-start | bytes 1769480 | tf_op jit(solution)/shard_map/ppermute | solution.py:722
  231.2 51.9 %collective-permute-start.13 = (bf16[2,576,256]{2,1,0:T(8,128)(2,1)}, bf16[2,576,256]{2,1,0:T(8,128)(2,1)S(1)}, u32[]{:S(2)}, u32[]{:S(2)}) collective-permute-start(bf16[2,576,256]{2,1,0:T(8,128)(2,1)} %get-tuple-element.73), channel_id=1, source_target_pairs={{0,8},{8,0},{16,24},{24,16},{1,9},{9,1},{17,25},{25,17},{2,10},{10... | collective-permute-start | bytes 1769480 | tf_op jit(solution)/shard_map/ppermute | solution.py:722
  232.6 60.3 %copy-start.18 = (bf16[736,128]{1,0:T(8,128)(2,1)}, bf16[736,128]{1,0:T(8,128)(2,1)S(1)}, u32[]{:S(2)}) copy-start(bf16[736,128]{1,0:T(8,128)(2,1)S(1)} %add_convert_fusion.4.refs_0_) | copy-start | bytes 565252
  232.6 50.6 %collective-permute-start.14 = (bf16[2,576,256]{2,1,0:T(8,128)(2,1)}, bf16[2,576,256]{2,1,0:T(8,128)(2,1)S(1)}, u32[]{:S(2)}, u32[]{:S(2)}) collective-permute-start(bf16[2,576,256]{2,1,0:T(8,128)(2,1)} %get-tuple-element.74), channel_id=1, source_target_pairs={{0,16},{8,24},{16,0},{24,8},{1,17},{9,25},{17,1},{25,9},{2,18},{10... | collective-permute-start | bytes 1769480 | tf_op jit(solution)/shard_map/ppermute | solution.py:722
  233.1 51.2 %collective-permute-start.15 = (bf16[2,576,256]{2,1,0:T(8,128)(2,1)}, bf16[2,576,256]{2,1,0:T(8,128)(2,1)S(1)}, u32[]{:S(2)}, u32[]{:S(2)}) collective-permute-start(bf16[2,576,256]{2,1,0:T(8,128)(2,1)} %get-tuple-element.75), channel_id=1, source_target_pairs={{0,24},{8,16},{16,8},{24,0},{1,25},{9,17},{17,9},{25,1},{2,26},{10... | collective-permute-start | bytes 1769480 | tf_op jit(solution)/shard_map/ppermute | solution.py:722
  236.1 9.7 %collective-permute-start.19 = (bf16[736,128]{1,0:T(8,128)(2,1)S(1)}, bf16[736,128]{1,0:T(8,128)(2,1)S(1)}, u32[]{:S(2)}, u32[]{:S(2)}) collective-permute-start(bf16[736,128]{1,0:T(8,128)(2,1)S(1)} %add_convert_fusion.4.refs_0_), channel_id=1, source_target_pairs={{0,2},{1,3},{2,0},{3,1},{4,6},{5,7},{6,4},{7,5},{8,10},{9,11},{10,... | collective-permute-start | bytes 565256 | tf_op jit(solution)/shard_map/ppermute | solution.py:609
  245.6 42.0 %copy-start.20 = (bf16[2,576,256]{2,1,0:T(8,128)(2,1)}, bf16[2,576,256]{2,1,0:T(8,128)(2,1)S(1)}, u32[]{:S(2)}) copy-start(bf16[2,576,256]{2,1,0:T(8,128)(2,1)S(1)} %collective-permute-done.8.refs_3_) | copy-start | bytes 1769476
  245.6 27.2 %collective-permute-start.23 = (bf16[576,128]{1,0:T(8,128)(2,1)S(1)}, bf16[576,128]{1,0:T(8,128)(2,1)S(1)}, u32[]{:S(2)}, u32[]{:S(2)}) collective-permute-start(bf16[576,128]{1,0:T(8,128)(2,1)S(1)} %get-tuple-element.99), channel_id=1, source_target_pairs={{0,8},{8,0},{16,24},{24,16},{1,9},{9,1},{17,25},{25,17},{2,10},{10... | collective-permute-start | bytes 442376 | tf_op jit(solution)/shard_map/ppermute | solution.py:605
  245.7 47.1 %copy-start.25 = (bf16[736,128]{1,0:T(8,128)(2,1)}, bf16[736,128]{1,0:T(8,128)(2,1)S(1)}, u32[]{:S(2)}) copy-start(bf16[736,128]{1,0:T(8,128)(2,1)S(1)} %collective-permute-done.19.refs_1_) | copy-start | bytes 565252
  245.7 27.4 %collective-permute-start.24 = (bf16[576,128]{1,0:T(8,128)(2,1)S(1)}, bf16[576,128]{1,0:T(8,128)(2,1)S(1)}, u32[]{:S(2)}, u32[]{:S(2)}) collective-permute-start(bf16[576,128]{1,0:T(8,128)(2,1)S(1)} %get-tuple-element.101), channel_id=1, source_target_pairs={{0,16},{8,24},{16,0},{24,8},{1,17},{9,25},{17,1},{25,9},{2,18},{10... | collective-permute-start | bytes 442376 | tf_op jit(solution)/shard_map/ppermute | solution.py:605
  272.8 6.0 %collective-permute-start.25 = (bf16[576,128]{1,0:T(8,128)(2,1)S(1)}, bf16[576,128]{1,0:T(8,128)(2,1)S(1)}, u32[]{:S(2)}, u32[]{:S(2)}) collective-permute-start(bf16[576,128]{1,0:T(8,128)(2,1)S(1)} %get-tuple-element.100), channel_id=1, source_target_pairs={{0,24},{8,16},{16,8},{24,0},{1,25},{9,17},{17,9},{25,1},{2,26},{10... | collective-permute-start | bytes 442376 | tf_op jit(solution)/shard_map/ppermute | solution.py:605
  273.1 25.0 %collective-permute-start.20 = (bf16[736,128]{1,0:T(8,128)(2,1)S(1)}, bf16[736,128]{1,0:T(8,128)(2,1)S(1)}, u32[]{:S(2)}, u32[]{:S(2)}) collective-permute-start(bf16[736,128]{1,0:T(8,128)(2,1)S(1)} %add_convert_fusion.4.refs_0_), channel_id=1, source_target_pairs={{0,4},{1,5},{2,6},{3,7},{4,0},{5,1},{6,2},{7,3},{8,12},{9,13},{10,... | collective-permute-start | bytes 565256 | tf_op jit(solution)/shard_map/ppermute | solution.py:609
  278.9 19.2 %collective-permute-start.21 = (bf16[736,128]{1,0:T(8,128)(2,1)S(1)}, bf16[736,128]{1,0:T(8,128)(2,1)S(1)}, u32[]{:S(2)}, u32[]{:S(2)}) collective-permute-start(bf16[736,128]{1,0:T(8,128)(2,1)S(1)} %add_convert_fusion.4.refs_0_), channel_id=1, source_target_pairs={{0,6},{1,7},{2,4},{3,5},{4,2},{5,3},{6,0},{7,1},{8,14},{9,15},{10,... | collective-permute-start | bytes 565256 | tf_op jit(solution)/shard_map/ppermute | solution.py:609
  283.1 9.7 %copy-start.21 = (bf16[2,576,256]{2,1,0:T(8,128)(2,1)}, bf16[2,576,256]{2,1,0:T(8,128)(2,1)S(1)}, u32[]{:S(2)}) copy-start(bf16[2,576,256]{2,1,0:T(8,128)(2,1)S(1)} %collective-permute-done.13.refs_1_) | copy-start | bytes 1769476
  283.1 19.1 %collective-permute-start.26 = (bf16[576,128]{1,0:T(8,128)(2,1)S(1)}, bf16[576,128]{1,0:T(8,128)(2,1)S(1)}, u32[]{:S(2)}, u32[]{:S(2)}) collective-permute-start(bf16[576,128]{1,0:T(8,128)(2,1)S(1)} %add_convert_fusion.10), channel_id=1, source_target_pairs={{0,2},{1,3},{2,0},{3,1},{4,6},{5,7},{6,4},{7,5},{8,10},{9,11},{10,... | collective-permute-start | bytes 442376 | tf_op jit(solution)/shard_map/ppermute | solution.py:609
  283.2 20.0 %collective-permute-start.27 = (bf16[576,128]{1,0:T(8,128)(2,1)S(1)}, bf16[576,128]{1,0:T(8,128)(2,1)S(1)}, u32[]{:S(2)}, u32[]{:S(2)}) collective-permute-start(bf16[576,128]{1,0:T(8,128)(2,1)S(1)} %add_convert_fusion.10), channel_id=1, source_target_pairs={{0,4},{1,5},{2,6},{3,7},{4,0},{5,1},{6,2},{7,3},{8,12},{9,13},{10,... | collective-permute-start | bytes 442376 | tf_op jit(solution)/shard_map/ppermute | solution.py:609
  284.4 18.9 %collective-permute-start.28 = (bf16[576,128]{1,0:T(8,128)(2,1)S(1)}, bf16[576,128]{1,0:T(8,128)(2,1)S(1)}, u32[]{:S(2)}, u32[]{:S(2)}) collective-permute-start(bf16[576,128]{1,0:T(8,128)(2,1)S(1)} %add_convert_fusion.10), channel_id=1, source_target_pairs={{0,6},{1,7},{2,4},{3,5},{4,2},{5,3},{6,0},{7,1},{8,14},{9,15},{10,... | collective-permute-start | bytes 442376 | tf_op jit(solution)/shard_map/ppermute | solution.py:609
  304.5 44.2 %copy-start = (bf16[3520,128]{1,0:T(8,128)(2,1)}, bf16[3520,128]{1,0:T(8,128)(2,1)S(1)}, u32[]{:S(2)}) copy-start(bf16[3520,128]{1,0:T(8,128)(2,1)S(1)} %pad_maximum_fusion.1.refs_0_) | copy-start | bytes 2703364
  304.5 23.0 %collective-permute-start.29 = (bf16[3520,128]{1,0:T(8,128)(2,1)S(1)}, bf16[3520,128]{1,0:T(8,128)(2,1)S(1)}, u32[]{:S(2)}, u32[]{:S(2)}) collective-permute-start(bf16[3520,128]{1,0:T(8,128)(2,1)S(1)} %pad_maximum_fusion.1.refs_0_), channel_id=1, source_target_pairs={{0,8},{8,0},{16,24},{24,16},{1,9},{9,1},{17,25},{25,17},{2,10},{10... | collective-permute-start | bytes 2703368 | tf_op jit(solution)/shard_map/ppermute | solution.py:605
  306.1 38.7 %collective-permute-start.30 = (bf16[3520,128]{1,0:T(8,128)(2,1)S(1)}, bf16[3520,128]{1,0:T(8,128)(2,1)S(1)}, u32[]{:S(2)}, u32[]{:S(2)}) collective-permute-start(bf16[3520,128]{1,0:T(8,128)(2,1)S(1)} %pad_maximum_fusion.1.refs_0_), channel_id=1, source_target_pairs={{0,16},{8,24},{16,0},{24,8},{1,17},{9,25},{17,1},{25,9},{2,18},{10... | collective-permute-start | bytes 2703368 | tf_op jit(solution)/shard_map/ppermute | solution.py:605
  307.8 37.0 %collective-permute-start.31 = (bf16[3520,128]{1,0:T(8,128)(2,1)S(1)}, bf16[3520,128]{1,0:T(8,128)(2,1)S(1)}, u32[]{:S(2)}, u32[]{:S(2)}) collective-permute-start(bf16[3520,128]{1,0:T(8,128)(2,1)S(1)} %pad_maximum_fusion.1.refs_0_), channel_id=1, source_target_pairs={{0,24},{8,16},{16,8},{24,0},{1,25},{9,17},{17,9},{25,1},{2,26},{10... | collective-permute-start | bytes 2703368 | tf_op jit(solution)/shard_map/ppermute | solution.py:605
  308.2 37.2 %collective-permute-start.32 = (bf16[3520,128]{1,0:T(8,128)(2,1)S(1)}, bf16[3520,128]{1,0:T(8,128)(2,1)S(1)}, u32[]{:S(2)}, u32[]{:S(2)}) collective-permute-start(bf16[3520,128]{1,0:T(8,128)(2,1)S(1)} %pad_maximum_fusion.1.refs_0_), channel_id=1, source_target_pairs={{0,1},{1,0},{2,3},{3,2},{4,5},{5,4},{6,7},{7,6},{8,9},{9,8},{10,11... | collective-permute-start | bytes 2703368 | tf_op jit(solution)/shard_map/ppermute | solution.py:602
  327.5 21.2 %copy-start.1 = (bf16[3520,128]{1,0:T(8,128)(2,1)}, bf16[3520,128]{1,0:T(8,128)(2,1)S(1)}, u32[]{:S(2)}) copy-start(bf16[3520,128]{1,0:T(8,128)(2,1)S(1)} %collective-permute-done.29.refs_1_) | copy-start | bytes 2703364
  327.5 17.8 %collective-permute-start.33 = (bf16[3520,128]{1,0:T(8,128)(2,1)S(1)}, bf16[3520,128]{1,0:T(8,128)(2,1)S(1)}, u32[]{:S(2)}, u32[]{:S(2)}) collective-permute-start(bf16[3520,128]{1,0:T(8,128)(2,1)S(1)} %collective-permute-done.29.refs_1_), channel_id=1, source_target_pairs={{0,1},{1,0},{2,3},{3,2},{4,5},{5,4},{6,7},{7,6},{8,9},{9,8},{10,11... | collective-permute-start | bytes 2703368 | tf_op jit(solution)/shard_map/ppermute | solution.py:602
  344.8 2.9 collective-permute-start.34
  344.9 3.9 %collective-permute-start.35 = (bf16[3520,128]{1,0:T(8,128)(2,1)S(1)}, bf16[3520,128]{1,0:T(8,128)(2,1)}, u32[]{:S(2)}, u32[]{:S(2)}) collective-permute-start(bf16[3520,128]{1,0:T(8,128)(2,1)S(1)} %collective-permute-done.31.refs_3_), channel_id=1, source_target_pairs={{0,1},{1,0},{2,3},{3,2},{4,5},{5,4},{6,7},{7,6},{8,9},{9,8},{10,11... | collective-permute-start | bytes 2703368 | tf_op jit(solution)/shard_map/ppermute | solution.py:602
  (20 other events, 71.3 us)
